TPU v7x, 512 devices: a whole 4x4x16 slice. The times are simulated.
512 devices in a mesh: depth: 64 (over x, z), rays: 8 (over y, core).
Axes of the slice: x: 4, y: 4, z: 16, core: 2. Of those that a mesh axis runs over, the one named last changes fastest.
Arguments:
- encoded: bfloat16 [64, 4, 4096, 256], P('depth', None, 'rays'), may hold values from -6 to 6
- deltas: float32 [64, 4, 4096], P('depth', None, 'rays'), may hold values from 0.00390625 to 0.03125
- w_in: bfloat16 [64, 256, 512], P('depth'), may hold values from -0.375 to 0.375
- w_mid: bfloat16 [64, 512, 512], P('depth'), may hold values from -0.25 to 0.25
- w_sigma: bfloat16 [64, 512], P('depth'), may hold values from -0.25 to 0.25
- order: int32 [8, 64], P('rays'), may hold values from 0 to 63, each once within a row
- target: bfloat16 [4096, 512], P('rays'), may hold values from -3 to 3
Outputs:
- grad_in: float32 [64, 256, 512], P('depth', 'rays')
- grad_mid: float32 [64, 512, 512], P('depth', 'rays')
- grad_sigma: float32 [64, 512], P('depth', 'rays')
- loss: float32 [], replicated
Inputs may be any that keep to these rules, and one draw needn't show every extreme that they name: Each row of order lists every region once.
All inputs are finite; a program needn't handle non-finite values.
Results may differ from a plain program's by a relative error of at most 0.015.
Values may be sent and summed in bfloat16 or wider, within the bound.
A program may use at most 64 MiB of HBM per device.

v0:
```python
import jax
import jax.numpy as jnp
from jax import lax
from jax.sharding import PartitionSpec as P


def contract_rows(left, right):
    return lax.dot_general(
        left, right, (((0,), (0,)), ((), ())), preferred_element_type=jnp.float32
    )


def body(encoded, deltas, w_in, w_mid, w_sigma, order, target):
    samples = encoded.shape[1]
    rays_dev = encoded.shape[2]
    width_in = encoded.shape[3]
    rows = encoded[0].reshape(samples * rays_dev, width_in)
    first = w_in[0]
    second = w_mid[0]
    density = w_sigma[0]
    spacing = deltas[0]
    hidden = jnp.maximum(jnp.dot(rows, first, preferred_element_type=jnp.float32), 0.0)
    hidden_b = hidden.astype(jnp.bfloat16)
    feat = jnp.dot(hidden_b, second, preferred_element_type=jnp.float32)
    logit = jnp.dot(hidden_b, density, preferred_element_type=jnp.float32)
    features = feat.shape[1]
    tau = jax.nn.softplus(logit).reshape(samples, rays_dev) * spacing
    excl = jnp.cumsum(tau, axis=0) - tau
    weight = jnp.exp(-excl) * (1.0 - jnp.exp(-tau))
    feat3 = feat.reshape(samples, rays_dev, features)
    segment = jnp.sum(weight[:, :, None] * feat3, axis=0)
    depth_tau = jnp.sum(tau, axis=0)
    regions = lax.axis_size("depth")
    region_me = lax.axis_index("depth")
    positions = jnp.arange(regions, dtype=jnp.int32)
    onehot = order[0][:, None] == positions[None, :]
    rank = jnp.sum(jnp.where(onehot, positions[:, None], 0), axis=0)
    rank_me = jnp.sum(jnp.where(positions == region_me, rank, 0))
    before = (rank < rank_me).astype(jnp.float32)
    after = (rank > rank_me).astype(jnp.float32)
    all_tau = lax.all_gather(depth_tau[None], "depth", axis=0, tiled=True)
    prefix = jnp.dot(before, all_tau, precision=lax.Precision.HIGHEST)
    trans = jnp.exp(-prefix)
    weighted = trans[:, None] * segment
    count_total = rays_dev * lax.axis_size("rays") * features
    color = lax.psum(weighted, "depth")
    err = color - target.astype(jnp.float32)
    loss = lax.psum(jnp.sum(err * err), "rays") / count_total
    dcolor = lax.optimization_barrier(err.astype(jnp.bfloat16)).astype(jnp.float32)
    qsum = jnp.sum(segment * dcolor, axis=1)
    all_terms = lax.all_gather((trans * qsum)[None], "depth", axis=0, tiled=True)
    gtau = -jnp.dot(after, all_terms, precision=lax.Precision.HIGHEST)
    dseg = trans[:, None] * dcolor
    dfeat = (weight[:, :, None] * dseg[None]).astype(jnp.bfloat16)
    vsum = jnp.sum(feat3 * dseg[None], axis=2)
    wv = weight * vsum
    dtau = (
        jnp.exp(-(excl + tau)) * vsum
        - (jnp.sum(wv, axis=0)[None] - jnp.cumsum(wv, axis=0))
        + gtau[None]
    )
    dz = (dtau * spacing).reshape(-1) * jax.nn.sigmoid(logit)
    dfeat2 = dfeat.reshape(samples * rays_dev, features)
    part_mid = contract_rows(hidden_b, dfeat2)
    part_sig = jnp.sum(hidden_b * dz[:, None], axis=0)
    dhb = lax.dot_general(
        dfeat2, second, (((1,), (1,)), ((), ())), preferred_element_type=jnp.float32
    )
    dhb = dhb + dz[:, None] * density.astype(jnp.float32)[None]
    dpre = jnp.where(hidden > 0, dhb, 0.0).astype(jnp.bfloat16)
    part_in = contract_rows(rows, dpre)
    grad_in, grad_mid, grad_sigma = (
        lax.psum_scatter(
            part_in.astype(jnp.bfloat16), "rays", scatter_dimension=0, tiled=True
        ).astype(jnp.float32),
        lax.psum_scatter(
            part_mid.astype(jnp.bfloat16), "rays", scatter_dimension=0, tiled=True
        ).astype(jnp.float32),
        lax.psum_scatter(
            part_sig.astype(jnp.bfloat16), "rays", scatter_dimension=0, tiled=True
        ).astype(jnp.float32),
    )
    return (grad_in[None], grad_mid[None], grad_sigma[None], loss)


def solution(mesh):
    in_specs = (
        P("depth", None, "rays", None),
        P("depth", None, "rays"),
        P("depth", None, None),
        P("depth", None, None),
        P("depth", None),
        P("rays", None),
        P("rays", None),
    )
    out_specs = (P("depth", "rays", None), P("depth", "rays", None), P("depth", "rays"), P())
    return jax.shard_map(body, mesh=mesh, in_specs=in_specs, out_specs=out_specs, check_vma=False)
```

profile of v0, /device:TPU:1, one launch (start us, length us, event | category | flops | bytes accessed | tf_op | source)
XLA Modules:
  0.0 593.9 jit_solution(4081673140898898454)
XLA Ops:
  7.2 1.2 copy-done
  8.4 3.6 maximum_convert_fusion
  12.8 80.8 %all-gather.2 = f32[64,1,512]{2,1,0:T(1,128)S(1)} all-gather(f32[1,1,512]{2,1,0:T(1,128)S(1)} %bitcast.96), channel_id=2, replica_groups=mesh['depth'=64,'rays'=8] {'depth'}, dimensions={0}, use_global_device_ids=true | all-gather | bytes 133120 | tf_op jit(solution)/shard_map/all_gather | solution.py:41
  95.2 4.5 multiply_reduce_fusion.2
  99.7 1.1 copy-done.2
  100.7 1.1 broadcast_multiply_fusion
  101.9 2.0 copy.25
  104.0 282.9 %all-reduce.3.cloned.1.call-done = f32[512,512]{0,1:T(8,128)} async-done(((f32[512,512]{0,1:T(8,128)}), f32[512,512]{0,1:T(8,128)}) %all-reduce.3.cloned.1.call-update) | async-done | bytes 1048592 | tf_op jit(solution)/shard_map/psum | solution.py:46
  386.9 2.4 multiply_reduce_fusion.3
  389.3 1.4 fusion.2
  390.7 2.2 multiply_reduce_fusion.1
  392.9 4.1 copy.26
  397.0 71.3 %all-gather.3 = f32[64,1,512]{2,1,0:T(1,128)S(1)} all-gather(f32[1,1,512]{2,1,0:T(1,128)S(1)} %bitcast.94), channel_id=3, replica_groups=mesh['depth'=64,'rays'=8] {'depth'}, dimensions={0}, use_global_device_ids=true | all-gather | bytes 133120 | tf_op jit(solution)/shard_map/all_gather | solution.py:51
  469.3 5.7 fusion.1
  475.0 0.9 copy.31
  475.9 2.6 copy.35
  478.5 1.6 fusion
  480.1 2.1 convolution_convert_fusion
  482.2 1.3 dynamic-slice
  484.1 48.9 %psum.15 = f32[]{:T(128)} all-reduce(f32[]{:T(128)} %get-tuple-element.24), channel_id=1, replica_groups=mesh['depth'=64,'rays'=8] {'rays'}, use_global_device_ids=true, to_apply=%region_15.16 | all-reduce | flops 1 | bytes 8 | tf_op jit(solution)/shard_map/psum | solution.py:48
  534.1 12.5 %all-reduce = bf16[512]{0:T(512)(128)(2,1)S(1)} all-reduce(bf16[512]{0:T(512)(128)(2,1)S(1)} %multiply_reduce_fusion), channel_id=6, replica_groups=mesh['depth'=64,'rays'=8] {'rays'}, use_global_device_ids=true, to_apply=%region_13.14.clone | all-reduce | flops 512 | bytes 2048
  547.2 0.9 copy.32
  548.8 35.9 %reduce-scatter.5.cloned.1.call-done = bf16[64,512]{1,0:T(8,128)(2,1)} async-done(((bf16[512,512]{1,0:T(8,128)(2,1)}), bf16[64,512]{1,0:T(8,128)(2,1)}) %reduce-scatter.5.cloned.1.call-update) | async-done | bytes 65552 | tf_op jit(solution)/shard_map/reduce_scatter | solution.py:76
  584.7 1.5 bitcast_convert_fusion.1
  (48 shorter events, 5.3 us)
Async XLA Ops:
  7.2 1.2 copy-start
  7.2 4.8 copy-start.5
  7.2 379.7 %all-reduce.3.cloned.1.call-start = ((), (), s32[]{:S(2)}) async-start(), calls=%async_computation.2 | async-start | bytes 2097152 | tf_op jit(solution)/shard_map/psum | solution.py:46
  8.4 4.3 copy-start.4
  8.4 85.2 %copy-start.6 = (s32[1,64]{1,0:T(1,128)S(1)}, s32[1,64]{1,0:T(1,128)}, u32[]{:S(2)}) copy-start(s32[1,64]{1,0:T(1,128)} %param.12) | copy-start | bytes 772
  99.7 1.1 copy-start.2
  101.9 445.3 %reduce-scatter.7.cloned.1.call-start = ((), (), s32[]{:S(2)}) async-start(), calls=%async_computation.4 | async-start | bytes 294912
  386.9 3.8 copy-start.1
  390.7 2.2 copy-start.3
  475.9 108.8 %reduce-scatter.5.cloned.1.call-start = ((), (), s32[]{:S(2)}) async-start(), calls=%async_computation.3 | async-start | bytes 589824 | tf_op jit(solution)/shard_map/reduce_scatter | solution.py:76
Sparse Core Ops, SparseCore 0:
  102.0 284.8 all-reduce.2
  476.0 68.3 reduce-scatter.6
  547.2 37.4 reduce-scatter.4
where the time goes:
time: 595 us; the launch traced here: 594 us
  waiting for transfers between devices  319 us (54%)
  blocking collectives  213 us (36%)
  matrix products  18.1 us (3%)
  between operations  16.3 us (3%)
  local copies, waits for them, and re-layouts  14.8 us (2%)
  other arithmetic  12.2 us (2%)
    psum x1, waiting for transfers between devices, body(): color = lax.psum(weighted, 'depth')  283 us
    all_gather x1, blocking collectives, body(): all_tau = lax.all_gather(depth_tau[None], 'depth', axis=0, tiled=True)  80.8 us
    all_gather x1, blocking collectives, body(): lax.all_gather((trans * qsum)[None], 'depth', axis=0, tiled=True)  71.3 us
    psum x1, blocking collectives, body(): loss = lax.psum(jnp.sum(err * err), 'rays') / count_total  48.9 us
    reduce_scatter x1, waiting for transfers between devices, body(): lax.psum_scatter(part_mid.astype(jnp.bfloat16), 'rays', scatter_dimension...  35.9 us
    unnamed x1, blocking collectives  12.5 us
  transfers between devices with their start and end apart: 3, of which 2 were waited for; matrix products, arithmetic and copies ran while one was open for 2% of the time, Pallas kernels for 0%

commit v1 on v0

v1 whole, which is shorter than its diff:
```python
import functools

import jax
import jax.numpy as jnp
from jax import lax
from jax.experimental import pallas as pl
from jax.experimental.pallas import tpu as pltpu
from jax.sharding import PartitionSpec as P

MESH = pl.DeviceIdType.MESH
XS, ZS, YS = 4, 16, 4
S = 4
Q = 128
E, H, F = 256, 512, 512
FB = 256
RB = 16
bf16, f32 = jnp.bfloat16, jnp.float32


def coords():
    d = lax.axis_index("depth")
    r = lax.axis_index("rays")
    return d // ZS, d % ZS, r // 2, r % 2


def device(x, z, y, c):
    return (x * ZS + z, y * 2 + c)


def remote(src, dst, send, recv, to):
    return pltpu.make_async_remote_copy(
        src_ref=src, dst_ref=dst, send_sem=send, recv_sem=recv, device_id=to, device_id_type=MESH
    )


def column(row):
    return jnp.transpose(jnp.broadcast_to(row, (Q, Q)))


def wide(a, n):
    return jnp.concatenate([a] * n, axis=1)


def stack(rows):
    at = lax.broadcasted_iota(jnp.int32, (8, Q), 0)
    out = jnp.zeros((8, Q), f32)
    for i, row in rows:
        out = jnp.where(at == i, row, out)
    return out


def far_first(i):
    k = (i + 1) // 2
    return ZS // 2 + k * (2 * (i % 2) - 1)


def kernel(
    enc, dlt, win_h, wmid_h, wsig, order, tgt,
    gi, gm, gs, loss,
    xb, win, wmid, tb, wsr, hid, hbt, xt, wrep, comp,
    sg_out, sg_in, tx_out, tx_in, tz, tr_out, tr_in,
    zs, zr, dc, uz, gx_out, gx_in,
    dsg, gg, vc, pmf, cm_out, cm_in, ym_own, ym_out, ym_in,
    pif, ci_out, ci_in, yi_own, yi_out, yi_in, sb, sc_in, sy_out, sy_in, dp,
    s_enc, s_w, sg_s, sg_r, tx_s, tx_r, tz_s, tz_r, tr_s, tr_r, zr_s, zr_r, za_s, za_r,
    xa_s, xa_r, uz_s, uz_r, gx_s, gx_r, c_s, c_r, ym_s, ym_r, yi_s, yi_r, sy_s, sy_r,
):
    x, z, y, c = coords()
    xd = lambda k: device((x + k) % XS, z, y, c)
    zd = lambda k: device(x, (z + k) % ZS, y, c)
    yd = lambda k: device(x, z, (y + k) % YS, c)
    other = device(x, z, y, 1 - c)
    zj, zh = z // 2, z % 2
    block = pl.ds(pl.multiple_of(zj * RB, RB), RB)

    def rays_of(d):
        return pl.multiple_of(((x + d) % XS) * Q, Q)

    load_in = pltpu.make_async_copy(win_h.at[0], win, s_w.at[0])
    load_in.start()

    def enc_copy(d):
        return pltpu.make_async_copy(enc.at[0, :, pl.ds(rays_of(d), Q), :], xb.at[d], s_enc.at[d])

    enc_copy(0).start()
    load_mid = pltpu.make_async_copy(wmid_h.at[0], wmid, s_w.at[1])
    load_mid.start()
    for d in range(1, XS):
        enc_copy(d).start()
    load_t = pltpu.make_async_copy(
        tgt.at[pl.ds(pl.multiple_of(x * Q + zj * RB, RB), RB), pl.ds(pl.multiple_of(zh * FB, FB), FB)], tb, s_w.at[2]
    )
    load_t.start()

    barrier = pltpu.get_barrier_semaphore()
    for k in range(1, XS):
        pl.semaphore_signal(barrier, inc=1, device_id=xd(k), device_id_type=MESH)
        pl.semaphore_signal(barrier, inc=1, device_id=yd(k), device_id_type=MESH)
    pl.semaphore_signal(barrier, inc=1, device_id=other, device_id_type=MESH)

    def greet(i, _):
        pl.semaphore_signal(barrier, inc=1, device_id=zd(far_first(i)), device_id_type=MESH)
        return 0

    lax.fori_loop(0, ZS - 1, greet, 0)

    eye = lax.broadcasted_iota(jnp.int32, (Q, Q), 0) == lax.broadcasted_iota(jnp.int32, (Q, Q), 1)
    sigma = wsig[...].astype(f32)
    for t in range(H // Q):
        wsr[t * Q:(t + 1) * Q, :] = column(sigma[:, t * Q:(t + 1) * Q]).astype(bf16)
    load_in.wait()

    def forward(d, _):
        enc_copy(d).wait()
        hp = jnp.dot(xb[d].reshape(S * Q, E), win[...], preferred_element_type=f32)
        h = jnp.maximum(hp, 0.0).astype(bf16)
        hid[d] = h
        lg = jnp.dot(h, wsr[...], preferred_element_type=f32)
        excl = jnp.zeros((1, Q), f32)
        hb = jnp.zeros((Q, H), f32)
        for k in range(S):
            logit = jnp.sum(jnp.where(eye, lg[k * Q:(k + 1) * Q], 0.0), axis=0, keepdims=True)
            delta = dlt[0, k:k + 1, pl.ds(rays_of(d), Q)]
            tau = (jnp.maximum(logit, 0.0) + jnp.log1p(jnp.exp(-jnp.abs(logit)))) * delta
            weight = jnp.exp(-excl) * (1.0 - jnp.exp(-tau))
            excl = excl + tau
            comp[d, k:k + 1, :] = weight
            comp[d, S + k:S + k + 1, :] = jnp.exp(-excl)
            comp[d, 2 * S + k:2 * S + k + 1, :] = delta / (1.0 + jnp.exp(-logit))
            wk = column(weight)
            wrep[d, k] = wk
            hb = hb + wide(wk, H // Q) * h[k * Q:(k + 1) * Q].astype(f32)
        tx_out[d] = stack([(0, excl)])
        hbt[d] = jnp.transpose(hb).astype(bf16)
        seg = jnp.dot(hb.astype(bf16), wmid[...], preferred_element_type=f32).astype(bf16)
        sg_out[d, 0] = seg[:, :FB]
        sg_out[d, 1] = seg[:, FB:]
        return 0

    load_mid.wait()
    lax.fori_loop(0, XS, forward, 0)

    pl.semaphore_wait(barrier, 2 * (XS - 1) + 1 + ZS - 1)

    def tx(k):
        return remote(tx_out.at[k], tx_in.at[k], tx_s.at[k], tx_r.at[k], xd(k))

    def sg(k, h):
        return remote(sg_out.at[k, h], sg_in.at[k, h], sg_s.at[k, h], sg_r.at[k, h], xd(k))

    for k in (2, 1, 3):
        tx(k).start()
    for h in range(2):
        for k in (2, 1, 3):
            sg(k, h).start()
    for k in (1, 3, 2):
        tx(k).wait_recv()
    tz[0] = stack([(0, tx_out[0, 0:1, :])] + [(k, tx_in[k, 0:1, :]) for k in range(1, XS)])

    def tz_copy(k):
        return remote(tz.at[0], tz.at[k], tz_s.at[k], tz_r.at[k], zd(k))

    lax.fori_loop(0, ZS - 1, lambda i, _: (tz_copy(far_first(i)).start(), 0)[1], 0)

    def turn(i, _):
        d, k = i // S, i % S
        t = jnp.transpose(xb[d, k].astype(f32)).astype(bf16)
        xt[d, :, pl.ds(pl.multiple_of(k * Q, Q), Q)] = t
        return 0

    lax.fori_loop(0, XS * S, turn, 0)
    row = lax.broadcasted_iota(jnp.int32, (ZS * 8, XS * ZS), 0)
    place = lax.broadcasted_iota(jnp.int32, (ZS * 8, XS * ZS), 1)
    region = ((x + XS - row % 8) % XS) * ZS + (z + ZS - row // 8) % ZS
    at = (region == order[...]) & (row % 8 < XS)
    rank = jnp.sum(jnp.where(at, place, 0).astype(f32), axis=1, keepdims=True)
    real = lax.broadcasted_iota(jnp.int32, (ZS * 8, 1), 0) % 8 < XS

    lax.fori_loop(1, ZS, lambda k, _: (tz_copy(k).wait_recv(), 0)[1], 0)
    taus = tz[...].reshape(ZS * 8, Q)
    trans = []
    for d in range(XS):
        front = (rank < rank[d:d + 1]) & real
        trans.append(jnp.exp(-jnp.sum(jnp.where(front, taus, 0.0), axis=0, keepdims=True)))
        tr_out[d] = stack([(0, trans[d])])

    def tr(k):
        return remote(tr_out.at[k], tr_in.at[k], tr_s.at[k], tr_r.at[k], xd(XS - k))

    for k in (2, 1, 3):
        tr(k).start()

    shade = [column(trans[d]) for d in range(XS)]
    for h in range(2):
        total = wide(shade[0], FB // Q) * sg_out[0, h].astype(f32)
        for k in range(1, XS):
            sg(k, h).wait_recv()
            total = total + wide(shade[k], FB // Q) * sg_in[k, h].astype(f32)
        zs[h] = total.astype(bf16)

    def zr_copy(k):
        to = (z + k) % ZS
        src = zs.at[to % 2, pl.ds(pl.multiple_of((to // 2) * RB, RB), RB), :]
        return remote(src, zr.at[k], zr_s.at[k], zr_r.at[k], zd(k))

    lax.fori_loop(0, ZS - 1, lambda i, _: (zr_copy(far_first(i)).start(), 0)[1], 0)
    zr[0] = zs[zh, block, :]
    load_t.wait()
    lax.fori_loop(1, ZS, lambda k, _: (zr_copy(k).wait_recv(), 0)[1], 0)
    color = jnp.sum(zr[...].astype(f32), axis=0)
    err = color - tb[...].astype(f32)
    square = jnp.sum(err * err, axis=0, keepdims=True)
    square = square[:, :Q] + square[:, Q:]
    dc[0, zh, block, :] = err.astype(bf16)

    def za_copy(k):
        ref = dc.at[0, zh, block, :]
        return remote(ref, ref, za_s.at[k], za_r.at[k], zd(k))

    lax.fori_loop(0, ZS - 1, lambda i, _: (za_copy(far_first(i)).start(), 0)[1], 0)

    def za_wait(k, _):
        at_z = (z + ZS - k) % ZS
        ref = dc.at[0, at_z % 2, pl.ds(pl.multiple_of((at_z // 2) * RB, RB), RB), :]
        remote(ref, ref, za_s.at[k], za_r.at[k], zd(k)).wait_recv()
        return 0

    lax.fori_loop(1, ZS, za_wait, 0)

    def xa(k, h):
        return remote(dc.at[0, h], dc.at[k, h], xa_s.at[k, h], xa_r.at[k, h], xd(XS - k))

    for h in range(2):
        for k in (2, 1, 3):
            xa(k, h).start()

    terms = []
    for d in range(XS):
        seg = sg_out if d == 0 else sg_in
        part = jnp.zeros((Q, Q), f32)
        for h in range(2):
            prod = seg[d, h].astype(f32) * dc[0, h].astype(f32)
            part = part + prod[:, :Q] + prod[:, Q:]
        terms.append(trans[d] * jnp.sum(jnp.transpose(part), axis=0, keepdims=True))
    uz[0] = stack(list(enumerate(terms)) + [(XS, square)])

    def uz_copy(k):
        return remote(uz.at[0], uz.at[k], uz_s.at[k], uz_r.at[k], zd(k))

    lax.fori_loop(0, ZS - 1, lambda i, _: (uz_copy(far_first(i)).start(), 0)[1], 0)

    for k in range(1, XS):
        tr(k).wait_recv()
    tr_in[0] = tr_out[0]

    def backward(d, _):
        @pl.when(d > 0)
        def _():
            for h in range(2):
                xa(d, h).wait_recv()

        t = wide(column(tr_in[d, 0:1, :]), F // Q)
        grad = jnp.concatenate([dc[d, 0], dc[d, 1]], axis=1).astype(f32)
        grad = (t * grad).astype(bf16)
        dsg[d] = grad
        g = lax.dot_general(grad, wmid[...], (((1,), (1,)), ((), ())), preferred_element_type=f32)
        gg[d] = g
        for k in range(S):
            prod = hid[d, k * Q:(k + 1) * Q, :].astype(f32) * g
            part = prod[:, :Q] + prod[:, Q:2 * Q] + prod[:, 2 * Q:3 * Q] + prod[:, 3 * Q:]
            vc[d, k:k + 1, :] = jnp.sum(jnp.transpose(part), axis=0, keepdims=True)
        return 0

    lax.fori_loop(0, XS, backward, 0)
    mid = jnp.dot(hbt[0], dsg[0], preferred_element_type=f32)
    for d in range(1, XS):
        mid = mid + jnp.dot(hbt[d], dsg[d], preferred_element_type=f32)
    pmf[...] = mid.reshape(YS, 2, H // (2 * YS), F)
    cm_out[...] = pmf[:, pl.ds(1 - c, 1)].reshape(YS, H // (2 * YS), F).astype(bf16)
    cm = remote(cm_out, cm_in, c_s.at[0], c_r.at[0], other)
    cm.start()

    lax.fori_loop(1, ZS, lambda k, _: (uz_copy(k).wait_recv(), 0)[1], 0)
    us = uz[...].reshape(ZS * 8, Q)
    squares = jnp.zeros((1, Q), f32)
    for k in range(ZS):
        squares = squares + uz[(z + ZS - k) % ZS, XS:XS + 1, :]
    for d in range(XS):
        behind = (rank > rank[d:d + 1]) & real
        back = -jnp.sum(jnp.where(behind, us, 0.0), axis=0, keepdims=True)
        gx_out[d] = stack([(0, back), (1, squares)])

    def gx(k):
        return remote(gx_out.at[k], gx_in.at[k], gx_s.at[k], gx_r.at[k], xd(XS - k))

    for k in (2, 1, 3):
        gx(k).start()
    gx_in[0] = gx_out[0]

    cm.wait_recv()
    own = pmf[:, pl.ds(c, 1)].reshape(YS, H // (2 * YS), F) + cm_in[...].astype(f32)
    ym_own[...] = own
    ym_out[...] = own.astype(bf16)

    def ym(k):
        return remote(ym_out.at[(y + k) % YS], ym_in.at[k], ym_s.at[k], ym_r.at[k], yd(k))

    for k in (2, 1, 3):
        ym(k).start()

    for k in (1, 3, 2):
        gx(k).wait_recv()
    pif[...] = jnp.zeros_like(pif)
    lines = sigma

    def finish(d, sig):
        gtau = gx_in[d, 0:1, :]
        later = jnp.zeros((1, Q), f32)
        g = gg[d]
        for k in reversed(range(S)):
            v = vc[d, k:k + 1, :]
            dtau = comp[d, S + k:S + k + 1, :] * v - later + gtau
            later = later + comp[d, k:k + 1, :] * v
            dz = wide(column(dtau * comp[d, 2 * S + k:2 * S + k + 1, :]), H // Q)
            h = hid[d, k * Q:(k + 1) * Q, :].astype(f32)
            pre = wide(wrep[d, k], H // Q) * g + dz * lines
            dp[k * Q:(k + 1) * Q, :] = jnp.where(h > 0.0, pre, 0.0).astype(bf16)
            sig = sig + jnp.sum((h * dz).reshape(Q // 8, 8, H), axis=0)
        pif[...] += jnp.dot(xt[d], dp[...], preferred_element_type=f32).reshape(pif.shape)
        return sig

    sig = lax.fori_loop(0, XS, finish, jnp.zeros((8, H), f32))
    sig = jnp.sum(sig, axis=0, keepdims=True)
    ci_out[...] = pif[:, pl.ds(1 - c, 1)].reshape(YS, E // (2 * YS), H).astype(bf16)
    ci = remote(ci_out, ci_in, c_s.at[1], c_r.at[1], other)
    ci.start()
    squares = jnp.zeros((1, Q), f32)
    for q in range(XS):
        squares = squares + gx_in[(q + XS - x) % XS, 1:2, :]
    sb[...] = stack([(t, sig[:, t * Q:(t + 1) * Q]) for t in range(H // Q)] + [(H // Q, squares)])
    sc = remote(sb, sc_in, c_s.at[2], c_r.at[2], other)
    sc.start()
    ci.wait_recv()
    own = pif[:, pl.ds(c, 1)].reshape(YS, E // (2 * YS), H) + ci_in[...].astype(f32)
    yi_own[...] = own
    yi_out[...] = own.astype(bf16)

    def yi(k):
        return remote(yi_out.at[(y + k) % YS], yi_in.at[k], yi_s.at[k], yi_r.at[k], yd(k))

    for k in (2, 1, 3):
        yi(k).start()
    sc.wait_recv()
    sy_out[...] = sb[...] + sc_in[...]
    sy_in[0] = sy_out[...]

    def sy(k):
        return remote(sy_out, sy_in.at[k], sy_s.at[k], sy_r.at[k], yd(k))

    for k in (2, 1, 3):
        sy(k).start()

    for k in range(1, YS):
        ym(k).wait_recv()
    total = ym_own[y]
    for k in range(1, YS):
        total = total + ym_in[k].astype(f32)
    gm[0] = total
    for k in range(1, YS):
        yi(k).wait_recv()
    total = yi_own[y]
    for k in range(1, YS):
        total = total + yi_in[k].astype(f32)
    gi[0] = total
    for k in range(1, YS):
        sy(k).wait_recv()
    total = jnp.zeros((8, Q), f32)
    for k in range(YS):
        total = total + sy_in[(y + YS - k) % YS]
    line = jnp.sum(jnp.where(lax.broadcasted_iota(jnp.int32, (8, Q), 0) == y, total, 0.0), axis=0, keepdims=True)
    gs[...] = jnp.where(c == 0, line[:, :Q // 2], line[:, Q // 2:])
    loss[0, 0] = jnp.sum(total[H // Q:H // Q + 1]) / (XS * Q * 2 * YS * F)

    for k in range(1, XS):
        tx(k).wait_send()
        tr(k).wait_send()
        gx(k).wait_send()
        ym(k).wait_send()
        yi(k).wait_send()
        sy(k).wait_send()
        for h in range(2):
            sg(k, h).wait_send()
            xa(k, h).wait_send()
    cm.wait_send()
    ci.wait_send()
    sc.wait_send()

    def sent(k, _):
        tz_copy(k).wait_send()
        zr_copy(k).wait_send()
        za_copy(k).wait_send()
        uz_copy(k).wait_send()
        return 0

    lax.fori_loop(1, ZS, sent, 0)


def body(encoded, deltas, w_in, w_mid, w_sigma, order, target):
    vm = pl.BlockSpec(memory_space=pltpu.VMEM)
    hbm = pl.BlockSpec(memory_space=pl.ANY)
    dma = pltpu.SemaphoreType.DMA
    v = pltpu.VMEM
    hm, hi = H // (2 * YS), E // (2 * YS)
    scratch = [
        v((XS, S, Q, E), bf16), v((E, H), bf16), v((H, F), bf16), v((RB, FB), bf16), v((H, Q), bf16),
        v((XS, S * Q, H), bf16), v((XS, H, Q), bf16), v((XS, E, S * Q), bf16), v((XS, S, Q, Q), f32), v((XS, 16, Q), f32),
        v((XS, 2, Q, FB), bf16), v((XS, 2, Q, FB), bf16), v((XS, 8, Q), f32), v((XS, 8, Q), f32), v((ZS, 8, Q), f32),
        v((XS, 8, Q), f32), v((XS, 8, Q), f32),
        v((2, Q, FB), bf16), v((ZS, RB, FB), bf16), v((XS, 2, Q, FB), bf16), v((ZS, 8, Q), f32),
        v((XS, 8, Q), f32), v((XS, 8, Q), f32),
        v((XS, Q, F), bf16), v((XS, Q, H), f32), v((XS, 8, Q), f32), v((YS, 2, hm, F), f32),
        v((YS, hm, F), bf16), v((YS, hm, F), bf16), v((YS, hm, F), f32), v((YS, hm, F), bf16), v((YS, hm, F), bf16),
        v((YS, 2, hi, H), f32),
        v((YS, hi, H), bf16), v((YS, hi, H), bf16), v((YS, hi, H), f32), v((YS, hi, H), bf16), v((YS, hi, H), bf16),
        v((8, Q), f32), v((8, Q), f32), v((8, Q), f32), v((YS, 8, Q), f32), v((S * Q, H), bf16),
        dma((XS,)), dma((3,)), dma((XS, 2)), dma((XS, 2)), dma((XS,)), dma((XS,)), dma((ZS,)), dma((ZS,)),
        dma((XS,)), dma((XS,)), dma((ZS,)), dma((ZS,)), dma((ZS,)), dma((ZS,)),
        dma((XS, 2)), dma((XS, 2)), dma((ZS,)), dma((ZS,)), dma((XS,)), dma((XS,)), dma((3,)), dma((3,)),
        dma((YS,)), dma((YS,)), dma((YS,)), dma((YS,)), dma((YS,)), dma((YS,)),
    ]
    grad_in, grad_mid, grad_sigma, loss = pl.pallas_call(
        kernel,
        out_shape=(
            jax.ShapeDtypeStruct((1, hi, H), f32),
            jax.ShapeDtypeStruct((1, hm, F), f32),
            jax.ShapeDtypeStruct((1, hm), f32),
            jax.ShapeDtypeStruct((1, 1), f32),
        ),
        in_specs=[hbm, vm, hbm, hbm, vm, vm, hbm],
        out_specs=(vm, vm, vm, pl.BlockSpec(memory_space=pltpu.SMEM)),
        scratch_shapes=scratch,
        compiler_params=pltpu.CompilerParams(collective_id=0, has_side_effects=True, vmem_limit_bytes=48 << 20),
        name="field_step",
    )(encoded, deltas, w_in, w_mid, w_sigma, order, target)
    return grad_in, grad_mid, grad_sigma, loss[0, 0]


def solution(mesh):
    in_specs = (
        P("depth", None, "rays", None),
        P("depth", None, "rays"),
        P("depth", None, None),
        P("depth", None, None),
        P("depth", None),
        P("rays", None),
        P("rays", None),
    )
    out_specs = (P("depth", "rays", None), P("depth", "rays", None), P("depth", "rays"), P())
    return jax.shard_map(body, mesh=mesh, in_specs=in_specs, out_specs=out_specs, check_vma=False)
```

time: 595 us -> 75 us (0.13)
  waiting for transfers between devices: 319 us -> 0 us
  blocking collectives: 213 us -> 0 us
  Pallas kernels: 0 us -> 64.2 us
  matrix products: 18.1 us -> 0 us
  between operations: 16.3 us -> 2.35 us
  other arithmetic: 12.2 us -> 0 us
  local copies, waits for them, and re-layouts: 14.8 us -> 8.08 us
    psum x1 -> x0, waiting for transfers between devices: 283 us -> none  [body(): color = lax.psum(weighted, 'depth')]
    all_gather x2 -> x0, blocking collectives: 152 us -> none  [the longest x1 80.8 us: body(): all_tau = lax.all_gather(depth_tau[None], 'depth', axis=0, tiled=True)]
    pallas_call x0 -> x1, Pallas kernels: none -> 64.2 us  [body(): pl.pallas_call(kernel, out_shape=(jax.ShapeDtypeStruct((1, hi, H), f32),...]
    psum x1 -> x0, blocking collectives: 48.9 us -> none  [body(): loss = lax.psum(jnp.sum(err * err), 'rays') / count_total]
    reduce_scatter x1 -> x0, waiting for transfers between devices: 35.9 us -> none  [body(): lax.psum_scatter(part_mid.astype(jnp.bfloat16), 'rays', scatter_dimension...]
    dot_general x7 -> x0, matrix products: 18.1 us -> none  [the longest x2 7.78 us: contract_rows(): lax.dot_general(left, right, (((0,), (0,)), ((), ())), preferred_element_...]
    unnamed x1 -> x0, blocking collectives: 12.5 us -> none
    reduce_sum x8 -> x0, other arithmetic: 7.23 us -> none  [the longest x1 2.39 us: body(): loss = lax.psum(jnp.sum(err * err), 'rays') / count_total]
  transfers between devices with their start and end apart: 3 -> 0, of which waited for: 2 -> 0; matrix products, arithmetic and copies ran while one was open for 2% -> 0% of each run, Pallas kernels for 0% -> 0%
where the time goes in v1:
time: 75 us; the launch traced here: 74.6 us
  Pallas kernels  64.2 us (86%)
  local copies, waits for them, and re-layouts  8.08 us (11%)
  between operations  2.35 us (3%)
    pallas_call x1, Pallas kernels, body(): pl.pallas_call(kernel, out_shape=(jax.ShapeDtypeStruct((1, hi, H), f32),...  64.2 us
    unnamed x17, local copies, waits for them, and re-layouts  8.08 us

profile of v1, /device:TPU:1, one launch (start us, length us, event | category | flops | bytes accessed | tf_op | source)
XLA Modules:
  0.0 74.6 jit_solution(12918103642604799346)
XLA Ops:
  0.6 0.0 copy-start
  0.6 1.2 %copy-done = bf16[1,4,512,256]{3,2,1,0:T(8,128)(2,1)S(1)} copy-done((bf16[1,4,512,256]{3,2,1,0:T(8,128)(2,1)S(1)}, bf16[1,4,512,256]{3,2,1,0:T(8,128)(2,1)}, u32[]{:S(2)}) %copy-start) | copy-done | bytes 1048600
  1.9 0.0 copy-start.1
  1.9 1.0 %copy-done.1 = bf16[1,512,512]{2,1,0:T(8,128)(2,1)S(1)} copy-done((bf16[1,512,512]{2,1,0:T(8,128)(2,1)S(1)}, bf16[1,512,512]{2,1,0:T(8,128)(2,1)}, u32[]{:S(2)}) %copy-start.1) | copy-done | bytes 524312
  2.9 0.0 copy-start.2
  2.9 1.0 %copy-done.2 = bf16[512,512]{1,0:T(8,128)(2,1)S(1)} copy-done((bf16[512,512]{1,0:T(8,128)(2,1)S(1)}, bf16[512,512]{1,0:T(8,128)(2,1)}, u32[]{:S(2)}) %copy-start.2) | copy-done | bytes 524312
  3.9 0.0 copy-start.3
  3.9 0.9 %copy-done.3 = bf16[1,256,512]{2,1,0:T(8,128)(2,1)S(1)} copy-done((bf16[1,256,512]{2,1,0:T(8,128)(2,1)S(1)}, bf16[1,256,512]{2,1,0:T(8,128)(2,1)}, u32[]{:S(2)}) %copy-start.3) | copy-done | bytes 262168
  4.9 0.0 copy-start.4
  4.9 0.7 copy-done.4
  5.6 0.0 copy-start.5
  5.6 0.7 copy-done.5
  6.3 0.0 copy-start.6
  6.3 0.7 copy-done.6
  6.9 64.2 %field_step.1 = (f32[1,32,512]{2,1,0:T(8,128)S(1)}, f32[1,64,512]{2,1,0:T(8,128)S(1)}, f32[1,64]{1,0:T(1,128)S(1)}, f32[1,1]{1,0:T(1,128)}) custom-call(bf16[1,4,512,256]{3,2,1,0:T(8,128)(2,1)S(1)} %copy-done, f32[1,4,512]{2,1,0:T(4,128)S(1)} %copy-done.4, bf16[1,256,512]{2,1,0:T(8,128)(2,1)S(1)} %copy-done.3, bf16[1,512,512]{2,1,0:T(8,128)(2,1)S(1)} %copy-done.1, ...), custom_call_target="tpu_custom_call" | custom-call | tf_op jit(solution)/shard_map/field_step/pallas_call | solution.py:431
  71.1 0.6 copy.15
  71.7 0.7 copy.16
  72.4 0.5 copy.17
Async XLA Ops:
  0.6 1.2 %copy-start = (bf16[1,4,512,256]{3,2,1,0:T(8,128)(2,1)S(1)}, bf16[1,4,512,256]{3,2,1,0:T(8,128)(2,1)}, u32[]{:S(2)}) copy-start(bf16[1,4,512,256]{3,2,1,0:T(8,128)(2,1)} %enc.1) | copy-start | bytes 3145732
  1.9 1.0 %copy-start.1 = (bf16[1,512,512]{2,1,0:T(8,128)(2,1)S(1)}, bf16[1,512,512]{2,1,0:T(8,128)(2,1)}, u32[]{:S(2)}) copy-start(bf16[1,512,512]{2,1,0:T(8,128)(2,1)} %wmid_h.1) | copy-start | bytes 1572868
  2.9 1.0 %copy-start.2 = (bf16[512,512]{1,0:T(8,128)(2,1)S(1)}, bf16[512,512]{1,0:T(8,128)(2,1)}, u32[]{:S(2)}) copy-start(bf16[512,512]{1,0:T(8,128)(2,1)} %tgt.1) | copy-start | bytes 1572868
  3.9 0.9 %copy-start.3 = (bf16[1,256,512]{2,1,0:T(8,128)(2,1)S(1)}, bf16[1,256,512]{2,1,0:T(8,128)(2,1)}, u32[]{:S(2)}) copy-start(bf16[1,256,512]{2,1,0:T(8,128)(2,1)} %win_h.1) | copy-start | bytes 786436
  4.9 0.7 copy-start.4
  5.6 0.7 copy-start.5
  6.3 0.7 copy-start.6

commit v2 on v1

--- a/solution.py
+++ b/solution.py
@@ -9,6 +9,8 @@
 
 MESH = pl.DeviceIdType.MESH
 XS, ZS, YS = 4, 16, 4
+ZP = ZS // 2
+G = 2 * XS
 S = 4
 Q = 128
 E, H, F = 256, 512, 512
@@ -49,33 +51,50 @@
     return out
 
 
-def far_first(i):
+def far_first(i, n):
     k = (i + 1) // 2
-    return ZS // 2 + k * (2 * (i % 2) - 1)
+    return n // 2 + k * (2 * (i % 2) - 1)
+
+
+def each(first, last, f):
+    def step(i, _):
+        f(i)
+        return 0
+
+    lax.fori_loop(first, last, step, 0)
 
 
 def kernel(
-    enc, dlt, win_h, wmid_h, wsig, order, tgt,
+    enc, dlt_h, win_h, wmid_h, wsig_h, order_h, tgt,
     gi, gm, gs, loss,
     xb, win, wmid, tb, wsr, hid, hbt, xt, wrep, comp,
     sg_out, sg_in, tx_out, tx_in, tz, tr_out, tr_in,
     zs, zr, dc, uz, gx_out, gx_in,
     dsg, gg, vc, pmf, cm_out, cm_in, ym_own, ym_out, ym_in,
-    pif, ci_out, ci_in, yi_own, yi_out, yi_in, sb, sc_in, sy_out, sy_in, dp,
+    pif, ci_out, ci_in, yi_own, yi_out, yi_in, sb, sc_in, sy_out, sy_in, dp, dlt, wsig, order,
     s_enc, s_w, sg_s, sg_r, tx_s, tx_r, tz_s, tz_r, tr_s, tr_r, zr_s, zr_r, za_s, za_r,
     xa_s, xa_r, uz_s, uz_r, gx_s, gx_r, c_s, c_r, ym_s, ym_r, yi_s, yi_r, sy_s, sy_r,
 ):
     x, z, y, c = coords()
     xd = lambda k: device((x + k) % XS, z, y, c)
-    zd = lambda k: device(x, (z + k) % ZS, y, c)
+    zd = lambda k: device(x, (z + 2 * k) % ZS, y, c)
     yd = lambda k: device(x, z, (y + k) % YS, c)
     other = device(x, z, y, 1 - c)
     zj, zh = z // 2, z % 2
+    pair = lambda e: z + e * (1 - 2 * zh)
+    ahead = lambda m: device((x + m // 2) % XS, pair(m % 2), y, c)
+    back = lambda m: device((x + XS - m // 2) % XS, pair(m % 2), y, c)
     block = pl.ds(pl.multiple_of(zj * RB, RB), RB)
 
     def rays_of(d):
         return pl.multiple_of(((x + d) % XS) * Q, Q)
 
+    load_s = pltpu.make_async_copy(wsig_h, wsig, s_w.at[3])
+    load_s.start()
+    load_d = pltpu.make_async_copy(dlt_h, dlt, s_w.at[4])
+    load_d.start()
+    load_o = pltpu.make_async_copy(order_h, order, s_w.at[5])
+    load_o.start()
     load_in = pltpu.make_async_copy(win_h.at[0], win, s_w.at[0])
     load_in.start()
 
@@ -93,18 +112,14 @@
     load_t.start()
 
     barrier = pltpu.get_barrier_semaphore()
-    for k in range(1, XS):
-        pl.semaphore_signal(barrier, inc=1, device_id=xd(k), device_id_type=MESH)
+    for k in range(1, YS):
         pl.semaphore_signal(barrier, inc=1, device_id=yd(k), device_id_type=MESH)
     pl.semaphore_signal(barrier, inc=1, device_id=other, device_id_type=MESH)
-
-    def greet(i, _):
-        pl.semaphore_signal(barrier, inc=1, device_id=zd(far_first(i)), device_id_type=MESH)
-        return 0
-
-    lax.fori_loop(0, ZS - 1, greet, 0)
+    each(0, ZP - 1, lambda i: pl.semaphore_signal(barrier, inc=1, device_id=zd(far_first(i, ZP)), device_id_type=MESH))
+    each(1, G, lambda m: pl.semaphore_signal(barrier, inc=1, device_id=ahead(m), device_id_type=MESH))
 
     eye = lax.broadcasted_iota(jnp.int32, (Q, Q), 0) == lax.broadcasted_iota(jnp.int32, (Q, Q), 1)
+    load_s.wait()
     sigma = wsig[...].astype(f32)
     for t in range(H // Q):
         wsr[t * Q:(t + 1) * Q, :] = column(sigma[:, t * Q:(t + 1) * Q]).astype(bf16)
@@ -138,29 +153,28 @@
         return 0
 
     load_mid.wait()
+    load_d.wait()
     lax.fori_loop(0, XS, forward, 0)
 
-    pl.semaphore_wait(barrier, 2 * (XS - 1) + 1 + ZS - 1)
-
-    def tx(k):
-        return remote(tx_out.at[k], tx_in.at[k], tx_s.at[k], tx_r.at[k], xd(k))
-
-    def sg(k, h):
-        return remote(sg_out.at[k, h], sg_in.at[k, h], sg_s.at[k, h], sg_r.at[k, h], xd(k))
-
-    for k in (2, 1, 3):
-        tx(k).start()
-    for h in range(2):
-        for k in (2, 1, 3):
-            sg(k, h).start()
-    for k in (1, 3, 2):
-        tx(k).wait_recv()
-    tz[0] = stack([(0, tx_out[0, 0:1, :])] + [(k, tx_in[k, 0:1, :]) for k in range(1, XS)])
+    pl.semaphore_wait(barrier, YS - 1 + 1 + ZP - 1 + G - 1)
+
+    def tx(m):
+        return remote(tx_out.at[m // 2], tx_in.at[m], tx_s.at[m], tx_r.at[m], ahead(m))
+
+    def sg(m):
+        return remote(sg_out.at[m // 2, (zh + m) % 2], sg_in.at[m], sg_s.at[m], sg_r.at[m], ahead(m))
+
+    each(1, G, lambda m: tx(m).start())
+    each(1, G, lambda m: sg(m).start())
+    tx_in[0] = tx_out[0]
+    sg_in[0] = sg_out[0, zh]
+    each(1, G, lambda m: tx(m).wait_recv())
+    tz[0] = stack([(m, tx_in[m, 0:1, :]) for m in range(G)])
 
     def tz_copy(k):
         return remote(tz.at[0], tz.at[k], tz_s.at[k], tz_r.at[k], zd(k))
 
-    lax.fori_loop(0, ZS - 1, lambda i, _: (tz_copy(far_first(i)).start(), 0)[1], 0)
+    each(0, ZP - 1, lambda i: tz_copy(far_first(i, ZP)).start())
 
     def turn(i, _):
         d, k = i // S, i % S
@@ -169,44 +183,43 @@
         return 0
 
     lax.fori_loop(0, XS * S, turn, 0)
-    row = lax.broadcasted_iota(jnp.int32, (ZS * 8, XS * ZS), 0)
-    place = lax.broadcasted_iota(jnp.int32, (ZS * 8, XS * ZS), 1)
-    region = ((x + XS - row % 8) % XS) * ZS + (z + ZS - row // 8) % ZS
-    at = (region == order[...]) & (row % 8 < XS)
-    rank = jnp.sum(jnp.where(at, place, 0).astype(f32), axis=1, keepdims=True)
-    real = lax.broadcasted_iota(jnp.int32, (ZS * 8, 1), 0) % 8 < XS
-
-    lax.fori_loop(1, ZS, lambda k, _: (tz_copy(k).wait_recv(), 0)[1], 0)
-    taus = tz[...].reshape(ZS * 8, Q)
+    load_o.wait()
+    row = lax.broadcasted_iota(jnp.int32, (XS * ZS, XS * ZS), 0)
+    place = lax.broadcasted_iota(jnp.int32, (XS * ZS, XS * ZS), 1)
+    at_z = (z + ZS - 2 * (row // G)) % ZS + (row % 2) * (1 - 2 * zh)
+    region = ((x + XS - row % G // 2) % XS) * ZS + at_z
+    rank = jnp.sum(jnp.where(region == order[...], place, 0).astype(f32), axis=1, keepdims=True)
+
+    each(1, ZP, lambda k: tz_copy(k).wait_recv())
+    taus = tz[...].reshape(XS * ZS, Q)
     trans = []
+    for m in range(G):
+        front = rank < rank[m:m + 1]
+        trans.append(jnp.exp(-jnp.sum(jnp.where(front, taus, 0.0), axis=0, keepdims=True)))
     for d in range(XS):
-        front = (rank < rank[d:d + 1]) & real
-        trans.append(jnp.exp(-jnp.sum(jnp.where(front, taus, 0.0), axis=0, keepdims=True)))
-        tr_out[d] = stack([(0, trans[d])])
+        tr_out[d] = stack([(0, trans[2 * d])])
 
     def tr(k):
-        return remote(tr_out.at[k], tr_in.at[k], tr_s.at[k], tr_r.at[k], xd(XS - k))
+        return remote(tr_out.at[k], tr_in.at[k], tr_s.at[k], tr_r.at[k], back(2 * k))
 
     for k in (2, 1, 3):
         tr(k).start()
 
-    shade = [column(trans[d]) for d in range(XS)]
-    for h in range(2):
-        total = wide(shade[0], FB // Q) * sg_out[0, h].astype(f32)
-        for k in range(1, XS):
-            sg(k, h).wait_recv()
-            total = total + wide(shade[k], FB // Q) * sg_in[k, h].astype(f32)
-        zs[h] = total.astype(bf16)
+    total = jnp.zeros((Q, FB), f32)
+    for m in range(G):
+        if m:
+            sg(m).wait_recv()
+        total = total + wide(column(trans[m]), FB // Q) * sg_in[m].astype(f32)
+    zs[...] = total.astype(bf16)
 
     def zr_copy(k):
-        to = (z + k) % ZS
-        src = zs.at[to % 2, pl.ds(pl.multiple_of((to // 2) * RB, RB), RB), :]
+        src = zs.at[pl.ds(pl.multiple_of(((zj + k) % ZP) * RB, RB), RB), :]
         return remote(src, zr.at[k], zr_s.at[k], zr_r.at[k], zd(k))
 
-    lax.fori_loop(0, ZS - 1, lambda i, _: (zr_copy(far_first(i)).start(), 0)[1], 0)
-    zr[0] = zs[zh, block, :]
+    each(0, ZP - 1, lambda i: zr_copy(far_first(i, ZP)).start())
+    zr[0] = zs[block, :]
     load_t.wait()
-    lax.fori_loop(1, ZS, lambda k, _: (zr_copy(k).wait_recv(), 0)[1], 0)
+    each(1, ZP, lambda k: zr_copy(k).wait_recv())
     color = jnp.sum(zr[...].astype(f32), axis=0)
     err = color - tb[...].astype(f32)
     square = jnp.sum(err * err, axis=0, keepdims=True)
@@ -217,37 +230,36 @@
         ref = dc.at[0, zh, block, :]
         return remote(ref, ref, za_s.at[k], za_r.at[k], zd(k))
 
-    lax.fori_loop(0, ZS - 1, lambda i, _: (za_copy(far_first(i)).start(), 0)[1], 0)
-
-    def za_wait(k, _):
-        at_z = (z + ZS - k) % ZS
-        ref = dc.at[0, at_z % 2, pl.ds(pl.multiple_of((at_z // 2) * RB, RB), RB), :]
+    each(0, ZP - 1, lambda i: za_copy(far_first(i, ZP)).start())
+
+    def za_wait(k):
+        ref = dc.at[0, zh, pl.ds(pl.multiple_of(((zj + ZP - k) % ZP) * RB, RB), RB), :]
         remote(ref, ref, za_s.at[k], za_r.at[k], zd(k)).wait_recv()
-        return 0
-
-    lax.fori_loop(1, ZS, za_wait, 0)
-
-    def xa(k, h):
-        return remote(dc.at[0, h], dc.at[k, h], xa_s.at[k, h], xa_r.at[k, h], xd(XS - k))
-
-    for h in range(2):
-        for k in (2, 1, 3):
-            xa(k, h).start()
-
+
+    each(1, ZP, za_wait)
+
+    def xa(m):
+        return remote(dc.at[0, zh], dc.at[m // 2, zh], xa_s.at[m], xa_r.at[m], back(m))
+
+    def xa_wait(m):
+        ref = dc.at[m // 2, (zh + m) % 2]
+        remote(ref, ref, xa_s.at[m], xa_r.at[m], back(m)).wait_recv()
+
+    each(1, G, lambda m: xa(m).start())
+
+    grad = dc[0, zh].astype(f32)
     terms = []
-    for d in range(XS):
-        seg = sg_out if d == 0 else sg_in
-        part = jnp.zeros((Q, Q), f32)
-        for h in range(2):
-            prod = seg[d, h].astype(f32) * dc[0, h].astype(f32)
-            part = part + prod[:, :Q] + prod[:, Q:]
-        terms.append(trans[d] * jnp.sum(jnp.transpose(part), axis=0, keepdims=True))
-    uz[0] = stack(list(enumerate(terms)) + [(XS, square)])
+    for m in range(G):
+        prod = sg_in[m].astype(f32) * grad
+        part = jnp.transpose(prod[:, :Q] + prod[:, Q:])
+        terms.append(trans[m] * jnp.sum(part, axis=0, keepdims=True))
+    uz[0, :G, :] = stack(list(enumerate(terms)))
+    uz[0, G:, :] = stack([(0, square)])
 
     def uz_copy(k):
         return remote(uz.at[0], uz.at[k], uz_s.at[k], uz_r.at[k], zd(k))
 
-    lax.fori_loop(0, ZS - 1, lambda i, _: (uz_copy(far_first(i)).start(), 0)[1], 0)
+    each(0, ZP - 1, lambda i: uz_copy(far_first(i, ZP)).start())
 
     for k in range(1, XS):
         tr(k).wait_recv()
@@ -256,8 +268,9 @@
     def backward(d, _):
         @pl.when(d > 0)
         def _():
-            for h in range(2):
-                xa(d, h).wait_recv()
+            xa_wait(2 * d)
+
+        xa_wait(2 * d + 1)
 
         t = wide(column(tr_in[d, 0:1, :]), F // Q)
         grad = jnp.concatenate([dc[d, 0], dc[d, 1]], axis=1).astype(f32)
@@ -280,21 +293,19 @@
     cm = remote(cm_out, cm_in, c_s.at[0], c_r.at[0], other)
     cm.start()
 
-    lax.fori_loop(1, ZS, lambda k, _: (uz_copy(k).wait_recv(), 0)[1], 0)
-    us = uz[...].reshape(ZS * 8, Q)
+    each(1, ZP, lambda k: uz_copy(k).wait_recv())
+    us = uz[:, :G, :].reshape(XS * ZS, Q)
     squares = jnp.zeros((1, Q), f32)
-    for k in range(ZS):
-        squares = squares + uz[(z + ZS - k) % ZS, XS:XS + 1, :]
-    for d in range(XS):
-        behind = (rank > rank[d:d + 1]) & real
-        back = -jnp.sum(jnp.where(behind, us, 0.0), axis=0, keepdims=True)
-        gx_out[d] = stack([(0, back), (1, squares)])
-
-    def gx(k):
-        return remote(gx_out.at[k], gx_in.at[k], gx_s.at[k], gx_r.at[k], xd(XS - k))
-
-    for k in (2, 1, 3):
-        gx(k).start()
+    for k in range(ZP):
+        squares = squares + uz[(zj + ZP - k) % ZP, G:G + 1, :]
+    for m in range(G):
+        behind = rank > rank[m:m + 1]
+        gx_out[m] = stack([(0, -jnp.sum(jnp.where(behind, us, 0.0), axis=0, keepdims=True)), (1, squares)])
+
+    def gx(m):
+        return remote(gx_out.at[m], gx_in.at[m], gx_s.at[m], gx_r.at[m], back(m))
+
+    each(1, G, lambda m: gx(m).start())
     gx_in[0] = gx_out[0]
 
     cm.wait_recv()
@@ -308,13 +319,12 @@
     for k in (2, 1, 3):
         ym(k).start()
 
-    for k in (1, 3, 2):
-        gx(k).wait_recv()
+    each(1, G, lambda m: gx(m).wait_recv())
     pif[...] = jnp.zeros_like(pif)
     lines = sigma
 
     def finish(d, sig):
-        gtau = gx_in[d, 0:1, :]
+        gtau = gx_in[2 * d, 0:1, :] + gx_in[2 * d + 1, 0:1, :]
         later = jnp.zeros((1, Q), f32)
         g = gg[d]
         for k in reversed(range(S)):
@@ -336,7 +346,8 @@
     ci.start()
     squares = jnp.zeros((1, Q), f32)
     for q in range(XS):
-        squares = squares + gx_in[(q + XS - x) % XS, 1:2, :]
+        for h in range(2):
+            squares = squares + gx_in[2 * ((q + XS - x) % XS) + (h + zh) % 2, 1:2, :]
     sb[...] = stack([(t, sig[:, t * Q:(t + 1) * Q]) for t in range(H // Q)] + [(H // Q, squares)])
     sc = remote(sb, sc_in, c_s.at[2], c_r.at[2], other)
     sc.start()
@@ -382,27 +393,36 @@
     loss[0, 0] = jnp.sum(total[H // Q:H // Q + 1]) / (XS * Q * 2 * YS * F)
 
     for k in range(1, XS):
-        tx(k).wait_send()
         tr(k).wait_send()
-        gx(k).wait_send()
         ym(k).wait_send()
         yi(k).wait_send()
         sy(k).wait_send()
-        for h in range(2):
-            sg(k, h).wait_send()
-            xa(k, h).wait_send()
     cm.wait_send()
     ci.wait_send()
     sc.wait_send()
 
-    def sent(k, _):
+    def sent_group(m):
+        tx(m).wait_send()
+        sg(m).wait_send()
+        xa(m).wait_send()
+        gx(m).wait_send()
+
+    each(1, G, sent_group)
+
+    def sent_z(k):
         tz_copy(k).wait_send()
         zr_copy(k).wait_send()
         za_copy(k).wait_send()
         uz_copy(k).wait_send()
-        return 0
-
-    lax.fori_loop(1, ZS, sent, 0)
+
+    each(1, ZP, sent_z)
+
+
+def settle(gi, gm, gs, loss, gi_o, gm_o, gs_o, loss_o):
+    gi_o[...] = gi[...]
+    gm_o[...] = gm[...]
+    gs_o[...] = gs[...]
+    loss_o[0, 0] = loss[0, 0]
 
 
 def body(encoded, deltas, w_in, w_mid, w_sigma, order, target):
@@ -414,18 +434,19 @@
     scratch = [
         v((XS, S, Q, E), bf16), v((E, H), bf16), v((H, F), bf16), v((RB, FB), bf16), v((H, Q), bf16),
         v((XS, S * Q, H), bf16), v((XS, H, Q), bf16), v((XS, E, S * Q), bf16), v((XS, S, Q, Q), f32), v((XS, 16, Q), f32),
-        v((XS, 2, Q, FB), bf16), v((XS, 2, Q, FB), bf16), v((XS, 8, Q), f32), v((XS, 8, Q), f32), v((ZS, 8, Q), f32),
+        v((XS, 2, Q, FB), bf16), v((G, Q, FB), bf16), v((XS, 8, Q), f32), v((G, 8, Q), f32), v((ZP, 8, Q), f32),
         v((XS, 8, Q), f32), v((XS, 8, Q), f32),
-        v((2, Q, FB), bf16), v((ZS, RB, FB), bf16), v((XS, 2, Q, FB), bf16), v((ZS, 8, Q), f32),
-        v((XS, 8, Q), f32), v((XS, 8, Q), f32),
+        v((Q, FB), bf16), v((ZP, RB, FB), bf16), v((XS, 2, Q, FB), bf16), v((ZP, 16, Q), f32),
+        v((G, 8, Q), f32), v((G, 8, Q), f32),
         v((XS, Q, F), bf16), v((XS, Q, H), f32), v((XS, 8, Q), f32), v((YS, 2, hm, F), f32),
         v((YS, hm, F), bf16), v((YS, hm, F), bf16), v((YS, hm, F), f32), v((YS, hm, F), bf16), v((YS, hm, F), bf16),
         v((YS, 2, hi, H), f32),
         v((YS, hi, H), bf16), v((YS, hi, H), bf16), v((YS, hi, H), f32), v((YS, hi, H), bf16), v((YS, hi, H), bf16),
         v((8, Q), f32), v((8, Q), f32), v((8, Q), f32), v((YS, 8, Q), f32), v((S * Q, H), bf16),
-        dma((XS,)), dma((3,)), dma((XS, 2)), dma((XS, 2)), dma((XS,)), dma((XS,)), dma((ZS,)), dma((ZS,)),
-        dma((XS,)), dma((XS,)), dma((ZS,)), dma((ZS,)), dma((ZS,)), dma((ZS,)),
-        dma((XS, 2)), dma((XS, 2)), dma((ZS,)), dma((ZS,)), dma((XS,)), dma((XS,)), dma((3,)), dma((3,)),
+        v((1, S, XS * Q), f32), v((1, H), bf16), v((1, XS * ZS), jnp.int32),
+        dma((XS,)), dma((6,)), dma((G,)), dma((G,)), dma((G,)), dma((G,)), dma((ZP,)), dma((ZP,)),
+        dma((XS,)), dma((XS,)), dma((ZP,)), dma((ZP,)), dma((ZP,)), dma((ZP,)),
+        dma((G,)), dma((G,)), dma((ZP,)), dma((ZP,)), dma((G,)), dma((G,)), dma((3,)), dma((3,)),
         dma((YS,)), dma((YS,)), dma((YS,)), dma((YS,)), dma((YS,)), dma((YS,)),
     ]
     grad_in, grad_mid, grad_sigma, loss = pl.pallas_call(
@@ -436,12 +457,21 @@
             jax.ShapeDtypeStruct((1, hm), f32),
             jax.ShapeDtypeStruct((1, 1), f32),
         ),
-        in_specs=[hbm, vm, hbm, hbm, vm, vm, hbm],
+        in_specs=[hbm] * 7,
         out_specs=(vm, vm, vm, pl.BlockSpec(memory_space=pltpu.SMEM)),
         scratch_shapes=scratch,
-        compiler_params=pltpu.CompilerParams(collective_id=0, has_side_effects=True, vmem_limit_bytes=48 << 20),
+        compiler_params=pltpu.CompilerParams(collective_id=0, has_side_effects=True, vmem_limit_bytes=60 << 20),
         name="field_step",
     )(encoded, deltas, w_in, w_mid, w_sigma, order, target)
+    smem = pl.BlockSpec(memory_space=pltpu.SMEM)
+    grad_in, grad_mid, grad_sigma, loss = pl.pallas_call(
+        settle,
+        out_shape=tuple(jax.ShapeDtypeStruct(a.shape, a.dtype) for a in (grad_in, grad_mid, grad_sigma, loss)),
+        in_specs=[vm] * 3 + [smem],
+        out_specs=(vm, vm, vm, smem),
+        compiler_params=pltpu.CompilerParams(vmem_limit_bytes=60 << 20),
+        name="settle",
+    )(grad_in, grad_mid, grad_sigma, loss)
     return grad_in, grad_mid, grad_sigma, loss[0, 0]
 
 

time: 75 us -> 73.2 us (0.976)
  Pallas kernels: 64.2 us -> 72.4 us
  local copies, waits for them, and re-layouts: 8.08 us -> 0 us
  between operations: 2.35 us -> 0.64 us
    unnamed x17 -> x0, local copies, waits for them, and re-layouts: 8.08 us -> none
    pallas_call x1, Pallas kernels: 64.2 us -> 70.2 us  [body(): pl.pallas_call(kernel, out_shape=(jax.ShapeDtypeStruct((1, hi, H), f32),...]
    pallas_call x0 -> x1, Pallas kernels: none -> 2.23 us  [body(): pl.pallas_call(settle, out_shape=tuple((jax.ShapeDtypeStruct(a.shape, a.d...]
where the time goes in v2:
time: 73.2 us; the launch traced here: 73 us
  Pallas kernels  72.4 us (99%)
    pallas_call x1, Pallas kernels, body(): pl.pallas_call(kernel, out_shape=(jax.ShapeDtypeStruct((1, hi, H), f32),...  70.2 us
    pallas_call x1, Pallas kernels, body(): pl.pallas_call(settle, out_shape=tuple((jax.ShapeDtypeStruct(a.shape, a.d...  2.23 us

profile of v2, /device:TPU:1, one launch (start us, length us, event | category | flops | bytes accessed | tf_op | source)
XLA Modules:
  0.0 73.0 jit_solution(1588258318260835616)
XLA Ops:
  0.6 70.2 %field_step.1 = (f32[1,32,512]{2,1,0:T(8,128)}, f32[1,64,512]{2,1,0:T(8,128)}, f32[1,64]{1,0:T(1,128)}, f32[1,1]{1,0:T(1,128)}) custom-call(bf16[1,4,512,256]{3,2,1,0:T(8,128)(2,1)} %enc.1, f32[1,4,512]{2,1,0:T(4,128)} %dlt_h.1, bf16[1,256,512]{2,1,0:T(8,128)(2,1)} %win_h.1, bf16[1,512,512]{2,1,0:T(8,128)(2,1)} %wmid_h.1, bf16[1,512]{1,0:T(2,128)(2,1)} %wsig_h.1, ...), custom_call_target="tpu_custom_call" | custom-call | tf_op jit(solution)/shard_map/field_step/pallas_call | solution.py:452
  70.8 2.2 %settle.1 = (f32[1,32,512]{2,1,0:T(8,128)}, f32[1,64,512]{2,1,0:T(8,128)}, f32[1,64]{1,0:T(1,128)}, f32[1,1]{1,0:T(1,128)}) custom-call(f32[1,32,512]{2,1,0:T(8,128)} %get-tuple-element.12.gi, f32[1,64,512]{2,1,0:T(8,128)} %get-tuple-element.13.gm, f32[1,64]{1,0:T(1,128)} %get-tuple-element.14.gs, f32[1,1]{1,0:T(1,128)} %get-tuple-element.15.loss), custom_call_target="tpu_custom_call" | custom-call | tf_op jit(solution)/shard_map/settle/pallas_call | solution.py:467

commit v3 on v2

--- a/solution.py
+++ b/solution.py
@@ -57,17 +57,14 @@
 
 
 def each(first, last, f):
-    def step(i, _):
+    for i in range(first, last):
         f(i)
-        return 0
-
-    lax.fori_loop(first, last, step, 0)
 
 
 def kernel(
     enc, dlt_h, win_h, wmid_h, wsig_h, order_h, tgt,
-    gi, gm, gs, loss,
-    xb, win, wmid, tb, wsr, hid, hbt, xt, wrep, comp,
+    gi_o, gm_o, gs_o, loss,
+    gi, gm, gs, xb, win, wmid, tb, wsr, hid, hbt, xt, wrep, comp,
     sg_out, sg_in, tx_out, tx_in, tz, tr_out, tr_in,
     zs, zr, dc, uz, gx_out, gx_in,
     dsg, gg, vc, pmf, cm_out, cm_in, ym_own, ym_out, ym_in,
@@ -98,12 +95,18 @@
     load_in = pltpu.make_async_copy(win_h.at[0], win, s_w.at[0])
     load_in.start()
 
+    def rows_of(d):
+        return pl.ds(d * Q if isinstance(d, int) else pl.multiple_of(d * Q, Q), Q)
+
     def enc_copy(d):
         return pltpu.make_async_copy(enc.at[0, :, pl.ds(rays_of(d), Q), :], xb.at[d], s_enc.at[d])
 
     enc_copy(0).start()
-    load_mid = pltpu.make_async_copy(wmid_h.at[0], wmid, s_w.at[1])
-    load_mid.start()
+    load_mid = [
+        pltpu.make_async_copy(wmid_h.at[0, :, pl.ds(h * FB, FB)], wmid.at[h], s_w.at[(1, 9)[h]]) for h in range(2)
+    ]
+    for h in range(2):
+        load_mid[h].start()
     for d in range(1, XS):
         enc_copy(d).start()
     load_t = pltpu.make_async_copy(
@@ -125,36 +128,38 @@
         wsr[t * Q:(t + 1) * Q, :] = column(sigma[:, t * Q:(t + 1) * Q]).astype(bf16)
     load_in.wait()
 
-    def forward(d, _):
+    load_d.wait()
+
+    def density(d, _):
         enc_copy(d).wait()
         hp = jnp.dot(xb[d].reshape(S * Q, E), win[...], preferred_element_type=f32)
         h = jnp.maximum(hp, 0.0).astype(bf16)
         hid[d] = h
         lg = jnp.dot(h, wsr[...], preferred_element_type=f32)
         excl = jnp.zeros((1, Q), f32)
-        hb = jnp.zeros((Q, H), f32)
         for k in range(S):
             logit = jnp.sum(jnp.where(eye, lg[k * Q:(k + 1) * Q], 0.0), axis=0, keepdims=True)
             delta = dlt[0, k:k + 1, pl.ds(rays_of(d), Q)]
             tau = (jnp.maximum(logit, 0.0) + jnp.log1p(jnp.exp(-jnp.abs(logit)))) * delta
-            weight = jnp.exp(-excl) * (1.0 - jnp.exp(-tau))
+            comp[d, k:k + 1, :] = jnp.exp(-excl) * (1.0 - jnp.exp(-tau))
             excl = excl + tau
-            comp[d, k:k + 1, :] = weight
             comp[d, S + k:S + k + 1, :] = jnp.exp(-excl)
             comp[d, 2 * S + k:2 * S + k + 1, :] = delta / (1.0 + jnp.exp(-logit))
-            wk = column(weight)
+        tx_out[d] = stack([(0, excl)])
+        return 0
+
+    lax.fori_loop(0, XS, density, 0)
+
+    def segments(d):
+        hb = jnp.zeros((Q, H), f32)
+        for k in range(S):
+            wk = column(comp[d, k:k + 1, :])
             wrep[d, k] = wk
-            hb = hb + wide(wk, H // Q) * h[k * Q:(k + 1) * Q].astype(f32)
-        tx_out[d] = stack([(0, excl)])
-        hbt[d] = jnp.transpose(hb).astype(bf16)
-        seg = jnp.dot(hb.astype(bf16), wmid[...], preferred_element_type=f32).astype(bf16)
-        sg_out[d, 0] = seg[:, :FB]
-        sg_out[d, 1] = seg[:, FB:]
-        return 0
-
-    load_mid.wait()
-    load_d.wait()
-    lax.fori_loop(0, XS, forward, 0)
+            hb = hb + wide(wk, H // Q) * hid[d, k * Q:(k + 1) * Q, :].astype(f32)
+        hb_b = hb.astype(bf16)
+        hbt[:, d * Q:(d + 1) * Q] = jnp.transpose(hb).astype(bf16)
+        for h in range(2):
+            sg_out[d, h] = jnp.dot(hb_b, wmid[h], preferred_element_type=f32).astype(bf16)
 
     pl.semaphore_wait(barrier, YS - 1 + 1 + ZP - 1 + G - 1)
 
@@ -164,10 +169,15 @@
     def sg(m):
         return remote(sg_out.at[m // 2, (zh + m) % 2], sg_in.at[m], sg_s.at[m], sg_r.at[m], ahead(m))
 
-    each(1, G, lambda m: tx(m).start())
-    each(1, G, lambda m: sg(m).start())
+    for m in (4, 5, 3, 7, 2, 6, 1):
+        tx(m).start()
     tx_in[0] = tx_out[0]
-    sg_in[0] = sg_out[0, zh]
+    for h in range(2):
+        load_mid[h].wait()
+    for d in (2, 1):
+        segments(d)
+        sg(2 * d).start()
+        sg(2 * d + 1).start()
     each(1, G, lambda m: tx(m).wait_recv())
     tz[0] = stack([(m, tx_in[m, 0:1, :]) for m in range(G)])
 
@@ -175,6 +185,12 @@
         return remote(tz.at[0], tz.at[k], tz_s.at[k], tz_r.at[k], zd(k))
 
     each(0, ZP - 1, lambda i: tz_copy(far_first(i, ZP)).start())
+    for d in (3, 0):
+        segments(d)
+        if d:
+            sg(2 * d).start()
+        sg(2 * d + 1).start()
+    sg_in[0] = sg_out[0, zh]
 
     def turn(i, _):
         d, k = i // S, i % S
@@ -239,13 +255,17 @@
     each(1, ZP, za_wait)
 
     def xa(m):
-        return remote(dc.at[0, zh], dc.at[m // 2, zh], xa_s.at[m], xa_r.at[m], back(m))
+        half = (zh + m) % 2
+        to = back(1) if m == 1 else back(m - m % 2)
+        at = zh if m == 1 else half
+        return remote(dc.at[0, at], dc.at[m // 2, at], xa_s.at[m], xa_r.at[m], to)
 
     def xa_wait(m):
         ref = dc.at[m // 2, (zh + m) % 2]
-        remote(ref, ref, xa_s.at[m], xa_r.at[m], back(m)).wait_recv()
-
-    each(1, G, lambda m: xa(m).start())
+        remote(ref, ref, xa_s.at[m], xa_r.at[m], back(1)).wait_recv()
+
+    for m in (1, 4, 2, 6):
+        xa(m).start()
 
     grad = dc[0, zh].astype(f32)
     terms = []
@@ -260,38 +280,46 @@
         return remote(uz.at[0], uz.at[k], uz_s.at[k], uz_r.at[k], zd(k))
 
     each(0, ZP - 1, lambda i: uz_copy(far_first(i, ZP)).start())
+    xa_wait(1)
+    for m in (5, 3, 7):
+        xa(m).start()
 
     for k in range(1, XS):
         tr(k).wait_recv()
     tr_in[0] = tr_out[0]
 
-    def backward(d, _):
-        @pl.when(d > 0)
-        def _():
-            xa_wait(2 * d)
-
-        xa_wait(2 * d + 1)
-
-        t = wide(column(tr_in[d, 0:1, :]), F // Q)
-        grad = jnp.concatenate([dc[d, 0], dc[d, 1]], axis=1).astype(f32)
-        grad = (t * grad).astype(bf16)
-        dsg[d] = grad
-        g = lax.dot_general(grad, wmid[...], (((1,), (1,)), ((), ())), preferred_element_type=f32)
-        gg[d] = g
-        for k in range(S):
-            prod = hid[d, k * Q:(k + 1) * Q, :].astype(f32) * g
-            part = prod[:, :Q] + prod[:, Q:2 * Q] + prod[:, 2 * Q:3 * Q] + prod[:, 3 * Q:]
-            vc[d, k:k + 1, :] = jnp.sum(jnp.transpose(part), axis=0, keepdims=True)
-        return 0
-
-    lax.fori_loop(0, XS, backward, 0)
-    mid = jnp.dot(hbt[0], dsg[0], preferred_element_type=f32)
-    for d in range(1, XS):
-        mid = mid + jnp.dot(hbt[d], dsg[d], preferred_element_type=f32)
-    pmf[...] = mid.reshape(YS, 2, H // (2 * YS), F)
-    cm_out[...] = pmf[:, pl.ds(1 - c, 1)].reshape(YS, H // (2 * YS), F).astype(bf16)
-    cm = remote(cm_out, cm_in, c_s.at[0], c_r.at[0], other)
-    cm.start()
+    def cm(t):
+        at = (zh + t) % 2
+        return remote(cm_out.at[at], cm_in.at[at], c_s.at[(0, 3)[t]], c_r.at[(0, 3)[t]], other)
+
+    def ym(t, k):
+        at = (zh + t) % 2
+        return remote(ym_out.at[at, (y + k) % YS], ym_in.at[at, k], ym_s.at[t, k], ym_r.at[t, k], yd(k))
+
+    def mid_start(t):
+        at = (zh + t) % 2
+        for d in range(XS):
+            if d:
+                xa_wait(2 * d + t)
+            shade = wide(column(tr_in[d, 0:1, :]), FB // Q)
+            dsg[at, d * Q:(d + 1) * Q, :] = (shade * dc[d, at].astype(f32)).astype(bf16)
+        mid = jnp.dot(hbt[...], dsg[at], preferred_element_type=f32)
+        pmf[at] = mid.reshape(YS, 2, H // (2 * YS), FB)
+        cm_out[at] = pmf[at, :, pl.ds(1 - c, 1)].reshape(YS, H // (2 * YS), FB).astype(bf16)
+        cm(t).start()
+        return lax.dot_general(dsg[at], wmid[at], (((1,), (1,)), ((), ())), preferred_element_type=f32)
+
+    def mid_sum(t):
+        at = (zh + t) % 2
+        cm(t).wait_recv()
+        own = pmf[at, :, pl.ds(c, 1)].reshape(YS, H // (2 * YS), FB) + cm_in[at].astype(f32)
+        ym_own[at] = own
+        ym_out[at] = own.astype(bf16)
+        for k in (2, 1, 3):
+            ym(t, k).start()
+
+    gg[...] = mid_start(0).reshape(XS, Q, H)
+    mid_sum(0)
 
     each(1, ZP, lambda k: uz_copy(k).wait_recv())
     us = uz[:, :G, :].reshape(XS * ZS, Q)
@@ -308,16 +336,18 @@
     each(1, G, lambda m: gx(m).start())
     gx_in[0] = gx_out[0]
 
-    cm.wait_recv()
-    own = pmf[:, pl.ds(c, 1)].reshape(YS, H // (2 * YS), F) + cm_in[...].astype(f32)
-    ym_own[...] = own
-    ym_out[...] = own.astype(bf16)
-
-    def ym(k):
-        return remote(ym_out.at[(y + k) % YS], ym_in.at[k], ym_s.at[k], ym_r.at[k], yd(k))
-
-    for k in (2, 1, 3):
-        ym(k).start()
+    gg[...] += mid_start(1).reshape(XS, Q, H)
+    mid_sum(1)
+
+    def inner(d, _):
+        g = gg[d]
+        for k in range(S):
+            prod = hid[d, k * Q:(k + 1) * Q, :].astype(f32) * g
+            part = prod[:, :Q] + prod[:, Q:2 * Q] + prod[:, 2 * Q:3 * Q] + prod[:, 3 * Q:]
+            vc[d, k:k + 1, :] = jnp.sum(jnp.transpose(part), axis=0, keepdims=True)
+        return 0
+
+    lax.fori_loop(0, XS, inner, 0)
 
     each(1, G, lambda m: gx(m).wait_recv())
     pif[...] = jnp.zeros_like(pif)
@@ -371,18 +401,24 @@
     for k in (2, 1, 3):
         sy(k).start()
 
-    for k in range(1, YS):
-        ym(k).wait_recv()
-    total = ym_own[y]
-    for k in range(1, YS):
-        total = total + ym_in[k].astype(f32)
-    gm[0] = total
+    for t in range(2):
+        for k in range(1, YS):
+            ym(t, k).wait_recv()
+    for h in range(2):
+        total = ym_own[h, y]
+        for k in range(1, YS):
+            total = total + ym_in[h, k].astype(f32)
+        gm[0, :, h * FB:(h + 1) * FB] = total
+    put_mid = pltpu.make_async_copy(gm, gm_o, s_w.at[6])
+    put_mid.start()
     for k in range(1, YS):
         yi(k).wait_recv()
     total = yi_own[y]
     for k in range(1, YS):
         total = total + yi_in[k].astype(f32)
     gi[0] = total
+    put_in = pltpu.make_async_copy(gi, gi_o, s_w.at[7])
+    put_in.start()
     for k in range(1, YS):
         sy(k).wait_recv()
     total = jnp.zeros((8, Q), f32)
@@ -390,14 +426,21 @@
         total = total + sy_in[(y + YS - k) % YS]
     line = jnp.sum(jnp.where(lax.broadcasted_iota(jnp.int32, (8, Q), 0) == y, total, 0.0), axis=0, keepdims=True)
     gs[...] = jnp.where(c == 0, line[:, :Q // 2], line[:, Q // 2:])
+    put_sig = pltpu.make_async_copy(gs, gs_o, s_w.at[8])
+    put_sig.start()
     loss[0, 0] = jnp.sum(total[H // Q:H // Q + 1]) / (XS * Q * 2 * YS * F)
 
+    put_mid.wait()
+    put_in.wait()
+    put_sig.wait()
     for k in range(1, XS):
         tr(k).wait_send()
-        ym(k).wait_send()
+        ym(0, k).wait_send()
+        ym(1, k).wait_send()
         yi(k).wait_send()
         sy(k).wait_send()
-    cm.wait_send()
+    cm(0).wait_send()
+    cm(1).wait_send()
     ci.wait_send()
     sc.wait_send()
 
@@ -426,28 +469,30 @@
 
 
 def body(encoded, deltas, w_in, w_mid, w_sigma, order, target):
+    hbm = pl.BlockSpec(memory_space=pl.ANY)
     vm = pl.BlockSpec(memory_space=pltpu.VMEM)
-    hbm = pl.BlockSpec(memory_space=pl.ANY)
     dma = pltpu.SemaphoreType.DMA
     v = pltpu.VMEM
     hm, hi = H // (2 * YS), E // (2 * YS)
     scratch = [
-        v((XS, S, Q, E), bf16), v((E, H), bf16), v((H, F), bf16), v((RB, FB), bf16), v((H, Q), bf16),
-        v((XS, S * Q, H), bf16), v((XS, H, Q), bf16), v((XS, E, S * Q), bf16), v((XS, S, Q, Q), f32), v((XS, 16, Q), f32),
+        v((1, hi, H), f32), v((1, hm, F), f32), v((1, hm), f32),
+        v((XS, S, Q, E), bf16), v((E, H), bf16), v((2, H, FB), bf16), v((RB, FB), bf16), v((H, Q), bf16),
+        v((XS, S * Q, H), bf16), v((H, XS * Q), bf16), v((XS, E, S * Q), bf16), v((XS, S, Q, Q), f32), v((XS, 16, Q), f32),
         v((XS, 2, Q, FB), bf16), v((G, Q, FB), bf16), v((XS, 8, Q), f32), v((G, 8, Q), f32), v((ZP, 8, Q), f32),
         v((XS, 8, Q), f32), v((XS, 8, Q), f32),
         v((Q, FB), bf16), v((ZP, RB, FB), bf16), v((XS, 2, Q, FB), bf16), v((ZP, 16, Q), f32),
         v((G, 8, Q), f32), v((G, 8, Q), f32),
-        v((XS, Q, F), bf16), v((XS, Q, H), f32), v((XS, 8, Q), f32), v((YS, 2, hm, F), f32),
-        v((YS, hm, F), bf16), v((YS, hm, F), bf16), v((YS, hm, F), f32), v((YS, hm, F), bf16), v((YS, hm, F), bf16),
+        v((2, XS * Q, FB), bf16), v((XS, Q, H), f32), v((XS, 8, Q), f32), v((2, YS, 2, hm, FB), f32),
+        v((2, YS, hm, FB), bf16), v((2, YS, hm, FB), bf16), v((2, YS, hm, FB), f32), v((2, YS, hm, FB), bf16),
+        v((2, YS, hm, FB), bf16),
         v((YS, 2, hi, H), f32),
         v((YS, hi, H), bf16), v((YS, hi, H), bf16), v((YS, hi, H), f32), v((YS, hi, H), bf16), v((YS, hi, H), bf16),
         v((8, Q), f32), v((8, Q), f32), v((8, Q), f32), v((YS, 8, Q), f32), v((S * Q, H), bf16),
         v((1, S, XS * Q), f32), v((1, H), bf16), v((1, XS * ZS), jnp.int32),
-        dma((XS,)), dma((6,)), dma((G,)), dma((G,)), dma((G,)), dma((G,)), dma((ZP,)), dma((ZP,)),
+        dma((XS,)), dma((10,)), dma((G,)), dma((G,)), dma((G,)), dma((G,)), dma((ZP,)), dma((ZP,)),
         dma((XS,)), dma((XS,)), dma((ZP,)), dma((ZP,)), dma((ZP,)), dma((ZP,)),
-        dma((G,)), dma((G,)), dma((ZP,)), dma((ZP,)), dma((G,)), dma((G,)), dma((3,)), dma((3,)),
-        dma((YS,)), dma((YS,)), dma((YS,)), dma((YS,)), dma((YS,)), dma((YS,)),
+        dma((G,)), dma((G,)), dma((ZP,)), dma((ZP,)), dma((G,)), dma((G,)), dma((4,)), dma((4,)),
+        dma((2, YS)), dma((2, YS)), dma((YS,)), dma((YS,)), dma((YS,)), dma((YS,)),
     ]
     grad_in, grad_mid, grad_sigma, loss = pl.pallas_call(
         kernel,
@@ -458,7 +503,7 @@
             jax.ShapeDtypeStruct((1, 1), f32),
         ),
         in_specs=[hbm] * 7,
-        out_specs=(vm, vm, vm, pl.BlockSpec(memory_space=pltpu.SMEM)),
+        out_specs=(hbm, hbm, hbm, pl.BlockSpec(memory_space=pltpu.SMEM)),
         scratch_shapes=scratch,
         compiler_params=pltpu.CompilerParams(collective_id=0, has_side_effects=True, vmem_limit_bytes=60 << 20),
         name="field_step",

time: 73.2 us -> 70.1 us (0.958)
  Pallas kernels: 72.4 us -> 69.3 us
    pallas_call x1, Pallas kernels: 70.2 us -> 67 us  [body(): pl.pallas_call(kernel, out_shape=(jax.ShapeDtypeStruct((1, hi, H), f32),...]
where the time goes in v3:
time: 70.1 us; the launch traced here: 69.9 us
  Pallas kernels  69.3 us (99%)
    pallas_call x1, Pallas kernels, body(): pl.pallas_call(kernel, out_shape=(jax.ShapeDtypeStruct((1, hi, H), f32),...  67 us
    pallas_call x1, Pallas kernels, body(): pl.pallas_call(settle, out_shape=tuple((jax.ShapeDtypeStruct(a.shape, a.d...  2.23 us

profile of v3, /device:TPU:1, one launch (start us, length us, event | category | flops | bytes accessed | tf_op | source)
XLA Modules:
  0.0 69.9 jit_solution(15243393678608481485)
XLA Ops:
  0.6 67.0 %field_step.1 = (f32[1,32,512]{2,1,0:T(8,128)}, f32[1,64,512]{2,1,0:T(8,128)}, f32[1,64]{1,0:T(1,128)}, f32[1,1]{1,0:T(1,128)}) custom-call(bf16[1,4,512,256]{3,2,1,0:T(8,128)(2,1)} %enc.1, f32[1,4,512]{2,1,0:T(4,128)} %dlt_h.1, bf16[1,256,512]{2,1,0:T(8,128)(2,1)} %win_h.1, bf16[1,512,512]{2,1,0:T(8,128)(2,1)} %wmid_h.1, bf16[1,512]{1,0:T(2,128)(2,1)} %wsig_h.1, ...), custom_call_target="tpu_custom_call" | custom-call | tf_op jit(solution)/shard_map/field_step/pallas_call | solution.py:497
  67.7 2.2 %settle.1 = (f32[1,32,512]{2,1,0:T(8,128)}, f32[1,64,512]{2,1,0:T(8,128)}, f32[1,64]{1,0:T(1,128)}, f32[1,1]{1,0:T(1,128)}) custom-call(f32[1,32,512]{2,1,0:T(8,128)} %get-tuple-element.12.gi, f32[1,64,512]{2,1,0:T(8,128)} %get-tuple-element.13.gm, f32[1,64]{1,0:T(1,128)} %get-tuple-element.14.gs, f32[1,1]{1,0:T(1,128)} %get-tuple-element.15.loss), custom_call_target="tpu_custom_call" | custom-call | tf_op jit(solution)/shard_map/settle/pallas_call | solution.py:512

commit v4 on v3

--- a/solution.py
+++ b/solution.py
@@ -15,6 +15,7 @@
 Q = 128
 E, H, F = 256, 512, 512
 FB = 256
+HB = 256
 RB = 16
 bf16, f32 = jnp.bfloat16, jnp.float32
 
@@ -68,7 +69,7 @@
     sg_out, sg_in, tx_out, tx_in, tz, tr_out, tr_in,
     zs, zr, dc, uz, gx_out, gx_in,
     dsg, gg, vc, pmf, cm_out, cm_in, ym_own, ym_out, ym_in,
-    pif, ci_out, ci_in, yi_own, yi_out, yi_in, sb, sc_in, sy_out, sy_in, dp, dlt, wsig, order,
+    pif, ci_out, ci_in, yi_own, yi_out, yi_in, sb, sc_in, sy_out, sy_in, dp, dzc, dlt, wsig, order,
     s_enc, s_w, sg_s, sg_r, tx_s, tx_r, tz_s, tz_r, tr_s, tr_r, zr_s, zr_r, za_s, za_r,
     xa_s, xa_r, uz_s, uz_r, gx_s, gx_r, c_s, c_r, ym_s, ym_r, yi_s, yi_r, sy_s, sy_r,
 ):
@@ -174,7 +175,7 @@
     tx_in[0] = tx_out[0]
     for h in range(2):
         load_mid[h].wait()
-    for d in (2, 1):
+    for d in (2,):
         segments(d)
         sg(2 * d).start()
         sg(2 * d + 1).start()
@@ -185,7 +186,7 @@
         return remote(tz.at[0], tz.at[k], tz_s.at[k], tz_r.at[k], zd(k))
 
     each(0, ZP - 1, lambda i: tz_copy(far_first(i, ZP)).start())
-    for d in (3, 0):
+    for d in (1, 3, 0):
         segments(d)
         if d:
             sg(2 * d).start()
@@ -333,7 +334,8 @@
     def gx(m):
         return remote(gx_out.at[m], gx_in.at[m], gx_s.at[m], gx_r.at[m], back(m))
 
-    each(1, G, lambda m: gx(m).start())
+    for m in (4, 5, 3, 7, 2, 6, 1):
+        gx(m).start()
     gx_in[0] = gx_out[0]
 
     gg[...] += mid_start(1).reshape(XS, Q, H)
@@ -351,29 +353,58 @@
 
     each(1, G, lambda m: gx(m).wait_recv())
     pif[...] = jnp.zeros_like(pif)
-    lines = sigma
-
-    def finish(d, sig):
-        gtau = gx_in[2 * d, 0:1, :] + gx_in[2 * d + 1, 0:1, :]
-        later = jnp.zeros((1, Q), f32)
-        g = gg[d]
-        for k in reversed(range(S)):
-            v = vc[d, k:k + 1, :]
-            dtau = comp[d, S + k:S + k + 1, :] * v - later + gtau
-            later = later + comp[d, k:k + 1, :] * v
-            dz = wide(column(dtau * comp[d, 2 * S + k:2 * S + k + 1, :]), H // Q)
-            h = hid[d, k * Q:(k + 1) * Q, :].astype(f32)
-            pre = wide(wrep[d, k], H // Q) * g + dz * lines
-            dp[k * Q:(k + 1) * Q, :] = jnp.where(h > 0.0, pre, 0.0).astype(bf16)
-            sig = sig + jnp.sum((h * dz).reshape(Q // 8, 8, H), axis=0)
-        pif[...] += jnp.dot(xt[d], dp[...], preferred_element_type=f32).reshape(pif.shape)
+
+    def finish(half):
+        cols = slice(half * HB, (half + 1) * HB)
+
+        def step(d, _):
+            if half == 0:
+                gtau = gx_in[2 * d, 0:1, :] + gx_in[2 * d + 1, 0:1, :]
+                later = jnp.zeros((1, Q), f32)
+                for k in reversed(range(S)):
+                    v = vc[d, k:k + 1, :]
+                    dtau = comp[d, S + k:S + k + 1, :] * v - later + gtau
+                    later = later + comp[d, k:k + 1, :] * v
+                    dzc[d, k] = column(dtau * comp[d, 2 * S + k:2 * S + k + 1, :])
+            for k in range(S):
+                h = hid[d, k * Q:(k + 1) * Q, cols]
+                pre = wide(wrep[d, k], HB // Q) * gg[d, :, cols] + wide(dzc[d, k], HB // Q) * sigma[:, cols]
+                dp[k * Q:(k + 1) * Q, :] = jnp.where(h > 0, pre, 0.0).astype(bf16)
+            pif[half] += jnp.dot(xt[d], dp[...], preferred_element_type=f32).reshape(YS, 2, E // (2 * YS), HB)
+            return 0
+
+        lax.fori_loop(0, XS, step, 0)
+        ci_out[half] = pif[half, :, pl.ds(1 - c, 1)].reshape(YS, E // (2 * YS), HB).astype(bf16)
+        ci(half).start()
+
+    def ci(half):
+        at = (1, 4)[half]
+        return remote(ci_out.at[half], ci_in.at[half], c_s.at[at], c_r.at[at], other)
+
+    def yi(half, k):
+        return remote(
+            yi_out.at[half, (y + k) % YS], yi_in.at[half, k], yi_s.at[half, k], yi_r.at[half, k], yd(k)
+        )
+
+    def in_sum(half):
+        ci(half).wait_recv()
+        own = pif[half, :, pl.ds(c, 1)].reshape(YS, E // (2 * YS), HB) + ci_in[half].astype(f32)
+        yi_own[half] = own
+        yi_out[half] = own.astype(bf16)
+        for k in (2, 1, 3):
+            yi(half, k).start()
+
+    finish(0)
+    finish(1)
+    in_sum(0)
+
+    def spread(d, sig):
+        for k in range(S):
+            prod = hid[d, k * Q:(k + 1) * Q, :].astype(f32) * wide(dzc[d, k], H // Q)
+            sig = sig + jnp.sum(prod.reshape(Q // 8, 8, H), axis=0)
         return sig
 
-    sig = lax.fori_loop(0, XS, finish, jnp.zeros((8, H), f32))
-    sig = jnp.sum(sig, axis=0, keepdims=True)
-    ci_out[...] = pif[:, pl.ds(1 - c, 1)].reshape(YS, E // (2 * YS), H).astype(bf16)
-    ci = remote(ci_out, ci_in, c_s.at[1], c_r.at[1], other)
-    ci.start()
+    sig = jnp.sum(lax.fori_loop(0, XS, spread, jnp.zeros((8, H), f32)), axis=0, keepdims=True)
     squares = jnp.zeros((1, Q), f32)
     for q in range(XS):
         for h in range(2):
@@ -381,16 +412,7 @@
     sb[...] = stack([(t, sig[:, t * Q:(t + 1) * Q]) for t in range(H // Q)] + [(H // Q, squares)])
     sc = remote(sb, sc_in, c_s.at[2], c_r.at[2], other)
     sc.start()
-    ci.wait_recv()
-    own = pif[:, pl.ds(c, 1)].reshape(YS, E // (2 * YS), H) + ci_in[...].astype(f32)
-    yi_own[...] = own
-    yi_out[...] = own.astype(bf16)
-
-    def yi(k):
-        return remote(yi_out.at[(y + k) % YS], yi_in.at[k], yi_s.at[k], yi_r.at[k], yd(k))
-
-    for k in (2, 1, 3):
-        yi(k).start()
+    in_sum(1)
     sc.wait_recv()
     sy_out[...] = sb[...] + sc_in[...]
     sy_in[0] = sy_out[...]
@@ -400,6 +422,32 @@
 
     for k in (2, 1, 3):
         sy(k).start()
+
+    for k in range(1, XS):
+        tr(k).wait_send()
+        ym(0, k).wait_send()
+        ym(1, k).wait_send()
+    cm(0).wait_send()
+    cm(1).wait_send()
+    ci(0).wait_send()
+    ci(1).wait_send()
+    sc.wait_send()
+
+    def sent_group(m):
+        tx(m).wait_send()
+        sg(m).wait_send()
+        xa(m).wait_send()
+        gx(m).wait_send()
+
+    each(1, G, sent_group)
+
+    def sent_z(k):
+        tz_copy(k).wait_send()
+        zr_copy(k).wait_send()
+        za_copy(k).wait_send()
+        uz_copy(k).wait_send()
+
+    each(1, ZP, sent_z)
 
     for t in range(2):
         for k in range(1, YS):
@@ -411,12 +459,12 @@
         gm[0, :, h * FB:(h + 1) * FB] = total
     put_mid = pltpu.make_async_copy(gm, gm_o, s_w.at[6])
     put_mid.start()
-    for k in range(1, YS):
-        yi(k).wait_recv()
-    total = yi_own[y]
-    for k in range(1, YS):
-        total = total + yi_in[k].astype(f32)
-    gi[0] = total
+    for h in range(2):
+        total = yi_own[h, y]
+        for k in range(1, YS):
+            yi(h, k).wait_recv()
+            total = total + yi_in[h, k].astype(f32)
+        gi[0, :, h * HB:(h + 1) * HB] = total
     put_in = pltpu.make_async_copy(gi, gi_o, s_w.at[7])
     put_in.start()
     for k in range(1, YS):
@@ -434,31 +482,9 @@
     put_in.wait()
     put_sig.wait()
     for k in range(1, XS):
-        tr(k).wait_send()
-        ym(0, k).wait_send()
-        ym(1, k).wait_send()
-        yi(k).wait_send()
+        yi(0, k).wait_send()
+        yi(1, k).wait_send()
         sy(k).wait_send()
-    cm(0).wait_send()
-    cm(1).wait_send()
-    ci.wait_send()
-    sc.wait_send()
-
-    def sent_group(m):
-        tx(m).wait_send()
-        sg(m).wait_send()
-        xa(m).wait_send()
-        gx(m).wait_send()
-
-    each(1, G, sent_group)
-
-    def sent_z(k):
-        tz_copy(k).wait_send()
-        zr_copy(k).wait_send()
-        za_copy(k).wait_send()
-        uz_copy(k).wait_send()
-
-    each(1, ZP, sent_z)
 
 
 def settle(gi, gm, gs, loss, gi_o, gm_o, gs_o, loss_o):
@@ -485,14 +511,15 @@
         v((2, XS * Q, FB), bf16), v((XS, Q, H), f32), v((XS, 8, Q), f32), v((2, YS, 2, hm, FB), f32),
         v((2, YS, hm, FB), bf16), v((2, YS, hm, FB), bf16), v((2, YS, hm, FB), f32), v((2, YS, hm, FB), bf16),
         v((2, YS, hm, FB), bf16),
-        v((YS, 2, hi, H), f32),
-        v((YS, hi, H), bf16), v((YS, hi, H), bf16), v((YS, hi, H), f32), v((YS, hi, H), bf16), v((YS, hi, H), bf16),
-        v((8, Q), f32), v((8, Q), f32), v((8, Q), f32), v((YS, 8, Q), f32), v((S * Q, H), bf16),
+        v((2, YS, 2, hi, HB), f32),
+        v((2, YS, hi, HB), bf16), v((2, YS, hi, HB), bf16), v((2, YS, hi, HB), f32), v((2, YS, hi, HB), bf16),
+        v((2, YS, hi, HB), bf16),
+        v((8, Q), f32), v((8, Q), f32), v((8, Q), f32), v((YS, 8, Q), f32), v((S * Q, HB), bf16), v((XS, S, Q, Q), f32),
         v((1, S, XS * Q), f32), v((1, H), bf16), v((1, XS * ZS), jnp.int32),
         dma((XS,)), dma((10,)), dma((G,)), dma((G,)), dma((G,)), dma((G,)), dma((ZP,)), dma((ZP,)),
         dma((XS,)), dma((XS,)), dma((ZP,)), dma((ZP,)), dma((ZP,)), dma((ZP,)),
-        dma((G,)), dma((G,)), dma((ZP,)), dma((ZP,)), dma((G,)), dma((G,)), dma((4,)), dma((4,)),
-        dma((2, YS)), dma((2, YS)), dma((YS,)), dma((YS,)), dma((YS,)), dma((YS,)),
+        dma((G,)), dma((G,)), dma((ZP,)), dma((ZP,)), dma((G,)), dma((G,)), dma((5,)), dma((5,)),
+        dma((2, YS)), dma((2, YS)), dma((2, YS)), dma((2, YS)), dma((YS,)), dma((YS,)),
     ]
     grad_in, grad_mid, grad_sigma, loss = pl.pallas_call(
         kernel,

time: 70.1 us -> 69 us (0.984)
  Pallas kernels: 69.3 us -> 68.2 us
    pallas_call x1, Pallas kernels: 67 us -> 65.9 us  [body(): pl.pallas_call(kernel, out_shape=(jax.ShapeDtypeStruct((1, hi, H), f32),...]
where the time goes in v4:
time: 69 us; the launch traced here: 68.8 us
  Pallas kernels  68.2 us (99%)
    pallas_call x1, Pallas kernels, body(): pl.pallas_call(kernel, out_shape=(jax.ShapeDtypeStruct((1, hi, H), f32),...  65.9 us
    pallas_call x1, Pallas kernels, body(): pl.pallas_call(settle, out_shape=tuple((jax.ShapeDtypeStruct(a.shape, a.d...  2.23 us

profile of v4, /device:TPU:1, one launch (start us, length us, event | category | flops | bytes accessed | tf_op | source)
XLA Modules:
  0.0 68.8 jit_solution(5050874870747122549)
XLA Ops:
  0.6 65.9 %field_step.1 = (f32[1,32,512]{2,1,0:T(8,128)}, f32[1,64,512]{2,1,0:T(8,128)}, f32[1,64]{1,0:T(1,128)}, f32[1,1]{1,0:T(1,128)}) custom-call(bf16[1,4,512,256]{3,2,1,0:T(8,128)(2,1)} %enc.1, f32[1,4,512]{2,1,0:T(4,128)} %dlt_h.1, bf16[1,256,512]{2,1,0:T(8,128)(2,1)} %win_h.1, bf16[1,512,512]{2,1,0:T(8,128)(2,1)} %wmid_h.1, bf16[1,512]{1,0:T(2,128)(2,1)} %wsig_h.1, ...), custom_call_target="tpu_custom_call" | custom-call | tf_op jit(solution)/shard_map/field_step/pallas_call | solution.py:524
  66.6 2.2 %settle.1 = (f32[1,32,512]{2,1,0:T(8,128)}, f32[1,64,512]{2,1,0:T(8,128)}, f32[1,64]{1,0:T(1,128)}, f32[1,1]{1,0:T(1,128)}) custom-call(f32[1,32,512]{2,1,0:T(8,128)} %get-tuple-element.12.gi, f32[1,64,512]{2,1,0:T(8,128)} %get-tuple-element.13.gm, f32[1,64]{1,0:T(1,128)} %get-tuple-element.14.gs, f32[1,1]{1,0:T(1,128)} %get-tuple-element.15.loss), custom_call_target="tpu_custom_call" | custom-call | tf_op jit(solution)/shard_map/settle/pallas_call | solution.py:539

commit v5 on v4

--- a/solution.py
+++ b/solution.py
@@ -175,10 +175,6 @@
     tx_in[0] = tx_out[0]
     for h in range(2):
         load_mid[h].wait()
-    for d in (2,):
-        segments(d)
-        sg(2 * d).start()
-        sg(2 * d + 1).start()
     each(1, G, lambda m: tx(m).wait_recv())
     tz[0] = stack([(m, tx_in[m, 0:1, :]) for m in range(G)])
 
@@ -186,7 +182,7 @@
         return remote(tz.at[0], tz.at[k], tz_s.at[k], tz_r.at[k], zd(k))
 
     each(0, ZP - 1, lambda i: tz_copy(far_first(i, ZP)).start())
-    for d in (1, 3, 0):
+    for d in (2, 1, 3, 0):
         segments(d)
         if d:
             sg(2 * d).start()

time: 69 us -> 69 us (level)
  no operation moved by 1% of the time
where the time goes in v5:
time: 69 us; the launch traced here: 68.8 us
  Pallas kernels  68.2 us (99%)
    pallas_call x1, Pallas kernels, body(): pl.pallas_call(kernel, out_shape=(jax.ShapeDtypeStruct((1, hi, H), f32),...  65.9 us
    pallas_call x1, Pallas kernels, body(): pl.pallas_call(settle, out_shape=tuple((jax.ShapeDtypeStruct(a.shape, a.d...  2.23 us

profile of v5, /device:TPU:1, one launch (start us, length us, event | category | flops | bytes accessed | tf_op | source)
XLA Modules:
  0.0 68.8 jit_solution(8737333812643830634)
XLA Ops:
  0.6 65.9 %field_step.1 = (f32[1,32,512]{2,1,0:T(8,128)}, f32[1,64,512]{2,1,0:T(8,128)}, f32[1,64]{1,0:T(1,128)}, f32[1,1]{1,0:T(1,128)}) custom-call(bf16[1,4,512,256]{3,2,1,0:T(8,128)(2,1)} %enc.1, f32[1,4,512]{2,1,0:T(4,128)} %dlt_h.1, bf16[1,256,512]{2,1,0:T(8,128)(2,1)} %win_h.1, bf16[1,512,512]{2,1,0:T(8,128)(2,1)} %wmid_h.1, bf16[1,512]{1,0:T(2,128)(2,1)} %wsig_h.1, ...), custom_call_target="tpu_custom_call" | custom-call | tf_op jit(solution)/shard_map/field_step/pallas_call | solution.py:520
  66.6 2.2 %settle.1 = (f32[1,32,512]{2,1,0:T(8,128)}, f32[1,64,512]{2,1,0:T(8,128)}, f32[1,64]{1,0:T(1,128)}, f32[1,1]{1,0:T(1,128)}) custom-call(f32[1,32,512]{2,1,0:T(8,128)} %get-tuple-element.12.gi, f32[1,64,512]{2,1,0:T(8,128)} %get-tuple-element.13.gm, f32[1,64]{1,0:T(1,128)} %get-tuple-element.14.gs, f32[1,1]{1,0:T(1,128)} %get-tuple-element.15.loss), custom_call_target="tpu_custom_call" | custom-call | tf_op jit(solution)/shard_map/settle/pallas_call | solution.py:535
